TPU v7x, 256 devices: a whole 4x4x8 slice. The times are simulated.
256 devices in a mesh: mem: 64 (over y, z, core), dp: 4 (over x).
Axes of the slice: x: 4, y: 4, z: 8, core: 2. Of those that a mesh axis runs over, the one named last changes fastest.
Arguments:
- picks: int32 [81920, 4], P(('mem', 'dp')), may hold values from 0 to 32767, as said below
- pick_weights: bfloat16 [81920, 4], P(('mem', 'dp')), may hold values from -4 to 4
- token_grads: bfloat16 [81920, 2048], P(('mem', 'dp')), may hold values from -6 to 6
- values: bfloat16 [32768, 512], P('mem'), may hold values from -6 to 6
- first_moment: float32 [32768, 512], P(('mem', 'dp')), may hold values from -1.5 to 1.5
- second_moment: float32 [32768, 512], P(('mem', 'dp')), may hold values from 0.01 to 1
- projectors: bfloat16 [4, 512, 2048], replicated, may hold values from -0.25 to 0.25
Outputs:
- layer_out: bfloat16 [81920, 2048], P(('mem', 'dp'))
- new_values: bfloat16 [32768, 512], P('mem')
- new_first: float32 [32768, 512], P(('mem', 'dp'))
- new_second: float32 [32768, 512], P(('mem', 'dp'))
Inputs may be any that keep to these rules, and one draw needn't show every extreme that they name: Among the picks of one device's tokens (rows of the same aligned block of 320 tokens) at most 40 fall into one range of 512 rows [o * 512, (o + 1) * 512); in every draw one such range receives exactly 40 picks from every block.
All inputs are finite; a program needn't handle non-finite values.
Results may differ from a plain program's by a relative error of at most 0.0055.
Values may be sent and summed in bfloat16 or wider, within the bound.
No kernel may reach another device: no remote copies, remote signals or barrier semaphores. Data moves between devices by JAX's collectives and lax.ppermute only.
A program may use at most 128 MiB of HBM per device.

v0:
```python
import jax
import jax.numpy as jnp
from jax import lax
from jax.sharding import PartitionSpec as P

beta_one = 0.9
beta_two = 0.999
corr_one = 1.0 - 0.9**50
corr_two = 1.0 - 0.999**50
learn_rate = 0.05
adam_eps = 1e-08


def adam_rows(old_rows, slab_grad, first_moment, second_moment):
    new_first = beta_one * first_moment + (1.0 - beta_one) * slab_grad
    new_second = beta_two * second_moment + (1.0 - beta_two) * slab_grad * slab_grad
    update_step = new_first / corr_one / (jnp.sqrt(new_second / corr_two) + adam_eps)
    updated = (old_rows.astype(jnp.float32) - learn_rate * update_step).astype(jnp.bfloat16)
    return (new_first, new_second, updated)


def on_device(picks, pick_weights, token_grads, values, first_moment, second_moment, projectors):
    owners = lax.axis_size("mem")
    rows_dev = values.shape[0]
    width = values.shape[1]
    tok_count, per_token = picks.shape
    proj_count = projectors.shape[0]
    out_width = projectors.shape[2]
    total_picks = tok_count * per_token
    capacity = 2 * total_picks // owners
    flat_picks = picks.reshape(-1)
    owner_ids = flat_picks // rows_dev
    local_rows = flat_picks - owner_ids * rows_dev
    member = (owner_ids[:, None] == jnp.arange(owners, dtype=jnp.int32)[None, :]).astype(jnp.int32)
    before = jnp.cumsum(member, axis=0) - member
    slot_ids = owner_ids * capacity + jnp.sum(before * member, axis=1)
    proj_ids = picks % proj_count
    flat_proj = projectors.reshape(proj_count * width, out_width)
    requests = jnp.zeros((owners * capacity,), jnp.int32).at[slot_ids].set(local_rows)
    requests = requests.reshape(owners, capacity)
    received = lax.all_to_all(requests, "mem", split_axis=0, concat_axis=0, tiled=True)
    looked = values[received]
    returned = lax.all_to_all(looked, "mem", split_axis=0, concat_axis=0, tiled=True)
    back_grads = lax.dot_general(
        token_grads, flat_proj, (((1,), (1,)), ((), ())), preferred_element_type=jnp.float32
    )
    back_grads = back_grads.astype(jnp.bfloat16).reshape(tok_count, proj_count, width)
    chosen = back_grads[jnp.arange(tok_count, dtype=jnp.int32)[:, None], proj_ids].reshape(
        total_picks, width
    )
    grad_rows = jnp.zeros((owners * capacity, width), jnp.bfloat16).at[slot_ids].set(chosen)
    grad_wts = (
        jnp.zeros((owners * capacity,), jnp.bfloat16).at[slot_ids].set(pick_weights.reshape(-1))
    )
    send_rows = grad_rows.reshape(owners, capacity, width)
    send_wts = grad_wts.reshape(owners, capacity)
    got_rows, got_wts = (
        lax.all_to_all(send_rows, "mem", split_axis=0, concat_axis=0, tiled=True),
        lax.all_to_all(send_wts, "mem", split_axis=0, concat_axis=0, tiled=True),
    )
    picked = returned.reshape(owners * capacity, width)[slot_ids].reshape(
        tok_count, per_token, width
    )
    mixing = jnp.where(
        proj_ids[..., None] == jnp.arange(proj_count, dtype=jnp.int32),
        pick_weights[..., None],
        jnp.zeros((), jnp.bfloat16),
    )
    proj_sums = jnp.einsum(
        "tjp,tjd->tpd", mixing, picked, preferred_element_type=jnp.float32
    ).astype(jnp.bfloat16)
    layer_out = jnp.dot(
        proj_sums.reshape(tok_count, proj_count * width),
        flat_proj,
        preferred_element_type=jnp.float32,
    ).astype(jnp.bfloat16)
    weighted = got_wts.astype(jnp.float32)[..., None] * got_rows.astype(jnp.float32)
    slab_grad = (
        jnp.zeros((rows_dev, width), jnp.float32)
        .at[received.reshape(-1)]
        .add(weighted.reshape(-1, width))
    )
    quarter = first_moment.shape[0]
    start = lax.axis_index("dp") * quarter
    share = lax.psum_scatter(slab_grad, "dp", scatter_dimension=0, tiled=True)
    old_rows = lax.dynamic_slice_in_dim(values, start, quarter, 0)
    new_first, new_second, new_part = adam_rows(old_rows, share, first_moment, second_moment)
    new_values = lax.all_gather(new_part, "dp", axis=0, tiled=True)
    return (layer_out, new_values, new_first, new_second)


def solution(mesh):
    placed = (
        P(("mem", "dp"), None),
        P(("mem", "dp"), None),
        P(("mem", "dp"), None),
        P("mem", None),
        P(("mem", "dp"), None),
        P(("mem", "dp"), None),
        P(),
    )
    return jax.shard_map(
        on_device,
        mesh=mesh,
        in_specs=placed,
        out_specs=(
            P(("mem", "dp"), None),
            P("mem", None),
            P(("mem", "dp"), None),
            P(("mem", "dp"), None),
        ),
        check_vma=False,
    )
```

profile of v0, /device:TPU:2, one launch (start us, length us, event | category | flops | bytes accessed | tf_op | source)
XLA Modules:
  0.0 281.6 jit_solution(2421176253188972156)
XLA Ops:
  7.2 0.0 copy-start
  7.2 0.9 copy.24
  8.1 0.1 reshape.239
  8.3 0.1 reshape.238
  8.4 0.1 reshape.237
  8.6 18.1 %reduce-window.6 = s32[64,10,128]{2,1,0:T(8,128)S(1)} reduce-window(s32[64,10,128]{2,1,0:T(8,128)S(1)} %fusion.8, s32[]{:T(128)} %constant.23.clone.1), window={size=1x1x128 pad=0_0x0_0x127_0}, to_apply=%region_0.1 | reduce-window | flops 10403840 | bytes 655364 | tf_op jit(solution)/shard_map/reduce-window
  26.7 0.2 slice.14
  26.9 0.3 copy.27
  27.2 0.1 copy.28
  27.3 0.2 broadcast_add_fusion
  27.6 0.2 copy.23
  27.7 0.2 reshape.285
  27.9 0.2 fusion.12
  28.1 12.6 %scatter_custom_fusion.1 = bf16[2560]{0:T(1024)(128)(2,1)S(1)} fusion(s32[1280]{0:T(1024)S(1)} %fusion.29, bf16[1280]{0:T(1024)(128)(2,1)S(1)} %reshape.285, bf16[]{:T(256)} %constant.26.clone.1), kind=kCustom, calls=%fused_computation.72 | custom fusion | bytes 5122 | tf_op jit(solution)/shard_map/scatter | solution.py:53
  40.8 0.7 all_to_all.27
  41.5 12.1 %all-to-all-start.2 = ((bf16[64,1,40]{2,1,0:T(2,128)(2,1)}), bf16[64,1,40]{2,1,0:T(2,128)(2,1)S(1)}, u32[]{:S(2)}, u32[]{:S(2)}) async-start(bf16[64,1,40]{2,1,0:T(2,128)(2,1)} %all_to_all.27), calls=%async_computation.2 | async-start | bytes 65536 | tf_op jit(solution)/shard_map/all_to_all | solution.py:59
  53.6 0.0 copy-start.4
  53.6 6.3 %convolution_convert_fusion = bf16[320,2048]{1,0:T(8,128)(2,1)S(1)} fusion(bf16[320,2048]{1,0:T(8,128)(2,1)S(1)} %copy-done, bf16[2048,2048]{1,0:T(8,128)(2,1)} %bitcast.51), kind=kOutput, calls=%fused_computation.10 | convolution fusion | flops 2685009920 | bytes 11010048 | tf_op jit(solution)/shard_map/dot_general | solution.py:44
  59.9 5.3 %scatter_custom_fusion = s32[2560]{0:T(1024)S(1)} fusion(s32[1280]{0:T(1024)S(1)} %fusion.29, s32[1280]{0:T(1024)S(1)} %get-tuple-element.9, s32[]{:T(128)} %constant.23.clone.1), kind=kCustom, calls=%fused_computation.69 | custom fusion | bytes 10244 | tf_op jit(solution)/shard_map/scatter | solution.py:39
  65.2 0.7 all_to_all.20
  65.9 10.5 %all-to-all-start = ((s32[64,1,40]{2,1,0:T(1,128)}), s32[64,1,40]{2,1,0:T(1,128)S(1)}, u32[]{:S(2)}, u32[]{:S(2)}) async-start(s32[64,1,40]{2,1,0:T(1,128)} %bitcast.2), calls=%async_computation | async-start | bytes 65536 | tf_op jit(solution)/shard_map/all_to_all | solution.py:41
  76.4 0.1 copy.33
  76.6 0.1 reshape.267
  76.7 1.8 reshape.246
  78.6 22.6 %scatter_custom_fusion.2 = bf16[2560,512]{1,0:T(8,128)(2,1)} fusion(s32[1280]{0:T(1024)S(1)} %fusion.29, bf16[320,4,512]{2,1,0:T(4,128)(2,1)} %reshape.246, s32[1280]{0:T(1024)S(1)} %reshape.267, bf16[]{:T(256)} %constant.26.clone.1), kind=kCustom, calls=%fused_computation.12 | custom fusion | bytes 2621952 | tf_op jit(solution)/shard_map/scatter | solution.py:51
  101.2 10.5 %all-to-all-start.3 = ((bf16[64,40,512]{2,1,0:T(8,128)(2,1)}), bf16[64,40,512]{2,1,0:T(8,128)(2,1)}, u32[]{:S(2)}, u32[]{:S(2)}) async-start(bf16[64,40,512]{2,1,0:T(8,128)(2,1)} %bitcast.43), calls=%async_computation.3 | async-start | bytes 5242880 | tf_op jit(solution)/shard_map/all_to_all | solution.py:58
  111.8 0.1 reshape.253
  111.9 8.2 %gather_fusion = bf16[2560,512]{1,0:T(8,128)(2,1)} fusion(bf16[512,512]{1,0:T(8,128)(2,1)S(1)} %copy-done.1, s32[3072]{0:T(1024)S(1)} %pad_clamp_fusion), kind=kCustom, calls=%fused_computation | custom fusion | bytes 5253120 | tf_op jit(solution)/shard_map/gather | solution.py:42
  120.1 53.3 %all-to-all-done.3 = bf16[64,40,512]{2,1,0:T(8,128)(2,1)} async-done(((bf16[64,40,512]{2,1,0:T(8,128)(2,1)}), bf16[64,40,512]{2,1,0:T(8,128)(2,1)}, u32[]{:S(2)}, u32[]{:S(2)}) %all-to-all-start.3) | async-done | bytes 2621472 | tf_op jit(solution)/shard_map/all_to_all | solution.py:58
  173.4 6.6 %all-to-all-start.1 = ((bf16[64,40,512]{2,1,0:T(8,128)(2,1)}), bf16[64,40,512]{2,1,0:T(8,128)(2,1)}, u32[]{:S(2)}, u32[]{:S(2)}) async-start(bf16[64,40,512]{2,1,0:T(8,128)(2,1)} %bitcast.44), calls=%async_computation.1 | async-start | bytes 5242880 | tf_op jit(solution)/shard_map/all_to_all | solution.py:43
  180.0 0.3 reduce-scatter.2.cloned.1.call-start
  180.3 0.5 broadcast.228
  180.8 0.7 reduce.7
  181.5 0.1 reshape.243
  181.7 4.5 %convert_multiply_fusion = f32[64,40,512]{2,1,0:T(8,128)} fusion(bf16[64,40,512]{2,1,0:T(8,128)(2,1)} %all-to-all-done.3, f32[64,40]{1,0:T(8,128)S(1)} %bitcast.48), kind=kLoop, calls=%fused_computation.7 | loop fusion | flops 2621440 | bytes 7874560 | tf_op jit(solution)/shard_map/mul | solution.py:77
  186.2 17.9 %scatter_custom_fusion.3 = f32[512,512]{1,0:T(8,128)} fusion(s32[2560]{0:T(1024)S(1)} %fusion.17, f32[2560,512]{1,0:T(8,128)} %bitcast.45, f32[]{:T(128)} %constant.73.clone.1), kind=kCustom, calls=%fused_computation.18 | custom fusion | flops 1310720 | bytes 1049088 | tf_op jit(solution)/shard_map/scatter-add | solution.py:81
  204.0 0.0 reduce-scatter.2.cloned.1.call-update
  204.1 0.1 copy.22
  204.2 37.4 %all-to-all-done.1 = bf16[64,40,512]{2,1,0:T(8,128)(2,1)} async-done(((bf16[64,40,512]{2,1,0:T(8,128)(2,1)}), bf16[64,40,512]{2,1,0:T(8,128)(2,1)}, u32[]{:S(2)}, u32[]{:S(2)}) %all-to-all-start.1) | async-done | bytes 2621472 | tf_op jit(solution)/shard_map/all_to_all | solution.py:43
  241.6 6.2 %gather_fusion.1 = bf16[1280,512]{1,0:T(8,128)(2,1)S(1)} fusion(bf16[2560,512]{1,0:T(8,128)(2,1)} %bitcast.5, s32[2048]{0:T(1024)S(1)} %pad_clamp_fusion.1), kind=kCustom, calls=%fused_computation.1 | custom fusion | bytes 2626560 | tf_op jit(solution)/shard_map/gather | solution.py:61
  247.9 1.2 reshape.242
  249.1 2.1 convolution_convert_fusion.1
  251.2 0.0 copy-start.2
  251.3 0.0 copy-start.3
  251.3 7.4 %fusion = bf16[320,2048]{1,0:T(8,128)(2,1)} fusion(bf16[4,512,2048]{2,1,0:T(8,128)(2,1)} %param.13, bf16[320,4,512]{2,1,0:T(4,128)(2,1)S(1)} %convolution_convert_fusion.1), kind=kOutput, calls=%fused_computation.9 | convolution fusion | flops 2685009920 | bytes 11010048 | tf_op jit(solution)/shard_map/dot_general | solution.py:72
  258.7 1.9 subtract_convert_fusion
  260.6 13.4 %all_gather.3 = bf16[512,512]{1,0:T(8,128)(2,1)S(1)} all-gather(bf16[128,512]{1,0:T(8,128)(2,1)S(1)} %get-tuple-element.4), channel_id=1, replica_groups=mesh['mem'=64,'dp'=4] {'dp'}, dimensions={0}, use_global_device_ids=true | all-gather | bytes 655360 | tf_op jit(solution)/shard_map/all_gather | solution.py:88
  274.0 0.8 copy.39
  (22 shorter events, 0.3 us)
Async XLA Ops:
  7.2 46.4 %copy-start = (bf16[320,2048]{1,0:T(8,128)(2,1)S(1)}, bf16[320,2048]{1,0:T(8,128)(2,1)}, u32[]{:S(2)}) copy-start(bf16[320,2048]{1,0:T(8,128)(2,1)} %param.9) | copy-start | bytes 3932164
  26.7 0.8 copy-start.5
  41.5 24.4 %all-to-all-start.2 = ((bf16[64,1,40]{2,1,0:T(2,128)(2,1)}), bf16[64,1,40]{2,1,0:T(2,128)(2,1)S(1)}, u32[]{:S(2)}, u32[]{:S(2)}) async-start(bf16[64,1,40]{2,1,0:T(2,128)(2,1)} %all_to_all.27), calls=%async_computation.2 | async-start | bytes 65536 | tf_op jit(solution)/shard_map/all_to_all | solution.py:59
  53.6 22.8 %copy-start.4 = (s32[320,4]{0,1:T(4,128)S(1)}, s32[320,4]{0,1:T(4,128)}, u32[]{:S(2)}) copy-start(s32[320,4]{0,1:T(4,128)} %param.7) | copy-start | bytes 15364
  65.9 35.3 %all-to-all-start = ((s32[64,1,40]{2,1,0:T(1,128)}), s32[64,1,40]{2,1,0:T(1,128)S(1)}, u32[]{:S(2)}, u32[]{:S(2)}) async-start(s32[64,1,40]{2,1,0:T(1,128)} %bitcast.2), calls=%async_computation | async-start | bytes 65536 | tf_op jit(solution)/shard_map/all_to_all | solution.py:41
  101.2 10.7 %copy-start.1 = (bf16[512,512]{1,0:T(8,128)(2,1)S(1)}, bf16[512,512]{1,0:T(8,128)(2,1)}, u32[]{:S(2)}) copy-start(bf16[512,512]{1,0:T(8,128)(2,1)} %param.10) | copy-start | bytes 1572868
  101.2 72.2 %all-to-all-start.3 = ((bf16[64,40,512]{2,1,0:T(8,128)(2,1)}), bf16[64,40,512]{2,1,0:T(8,128)(2,1)}, u32[]{:S(2)}, u32[]{:S(2)}) async-start(bf16[64,40,512]{2,1,0:T(8,128)(2,1)} %bitcast.43), calls=%async_computation.3 | async-start | bytes 5242880 | tf_op jit(solution)/shard_map/all_to_all | solution.py:58
  173.4 68.2 %all-to-all-start.1 = ((bf16[64,40,512]{2,1,0:T(8,128)(2,1)}), bf16[64,40,512]{2,1,0:T(8,128)(2,1)}, u32[]{:S(2)}, u32[]{:S(2)}) async-start(bf16[64,40,512]{2,1,0:T(8,128)(2,1)} %bitcast.44), calls=%async_computation.1 | async-start | bytes 5242880 | tf_op jit(solution)/shard_map/all_to_all | solution.py:43
  180.0 78.7 %reduce-scatter.2.cloned.1.call-start = ((), (), s32[]{:S(2)}) async-start(), calls=%async_computation.5 | async-start | bytes 1310720 | tf_op jit(solution)/shard_map/reduce_scatter | solution.py:85
  251.2 7.4 %copy-start.2 = (f32[128,512]{1,0:T(8,128)S(1)}, f32[128,512]{1,0:T(8,128)}, u32[]{:S(2)}) copy-start(f32[128,512]{1,0:T(8,128)} %param.11) | copy-start | bytes 786436
  251.3 7.4 %copy-start.3 = (f32[128,512]{1,0:T(8,128)S(1)}, f32[128,512]{1,0:T(8,128)}, u32[]{:S(2)}) copy-start(f32[128,512]{1,0:T(8,128)} %param.12) | copy-start | bytes 786436
Sparse Core Ops, SparseCore 0:
  204.2 24.8 reduce-scatter.1
where the time goes:
time: 282 us
  waiting for transfers between devices  90.8 us (32%)
  local copies, waits for them, and re-layouts  63.6 us (23%)
  other arithmetic  43.7 us (15%)
  starting transfers between devices  40 us (14%)
  matrix products  15.8 us (6%)
  between operations  14.3 us (5%)
  blocking collectives  13.4 us (5%)
    all_to_all x1, waiting for transfers between devices, on_device(): lax.all_to_all(send_rows, 'mem', split_axis=0, concat_axis=0, tiled=True)  53.3 us
    all_to_all x1, waiting for transfers between devices, on_device(): lax.all_to_all(looked, 'mem', split_axis=0, concat_axis=0, tiled=True)  37.4 us
    scatter x1, local copies, waits for them, and re-layouts, on_device(): jnp.zeros((owners * capacity, width), jnp.bfloat16).at[slot_ids].set(chosen)  22.6 us
    another operation x3, other arithmetic  18.4 us
    scatter-add x1, other arithmetic, on_device(): slab_grad = jnp.zeros((rows_dev, width), jnp.float32).at[received.reshape...  17.9 us
    all_gather x1, blocking collectives, on_device(): new_values = lax.all_gather(new_part, 'dp', axis=0, tiled=True)  13.4 us
    scatter x1, local copies, waits for them, and re-layouts, on_device(): jnp.zeros((owners * capacity,), jnp.bfloat16).at[slot_ids]  12.6 us
    all_to_all x1, starting transfers between devices, on_device(): lax.all_to_all(send_wts, 'mem', split_axis=0, concat_axis=0, tiled=True)  12.1 us
  transfers between devices with their start and end apart: 5, of which 2 were waited for; matrix products, arithmetic and copies ran while one was open for 30% of the time, Pallas kernels for 0%

commit v1 on v0

v1 whole, which is shorter than its diff:
```python
import functools

import jax
import jax.numpy as jnp
from jax import lax
from jax.experimental import pallas as pl
from jax.experimental.pallas import tpu as pltpu
from jax.sharding import Mesh
from jax.sharding import PartitionSpec as P

beta_one = 0.9
beta_two = 0.999
corr_one = 1.0 - 0.9**50
corr_two = 1.0 - 0.999**50
learn_rate = 0.05
adam_eps = 1e-08

Z_CHIPS = 8
CORES = 2
CAP = 80
LANES = 128
FLAG_ROWS = 16
VMEM = 56 * 1024 * 1024
BF = jnp.bfloat16
F32 = jnp.float32
NT = (((1,), (1,)), ((), ()))


def adam_rows(old_rows, slab_grad, first_moment, second_moment):
    new_first = beta_one * first_moment + (1.0 - beta_one) * slab_grad
    new_second = beta_two * second_moment + (1.0 - beta_two) * slab_grad * slab_grad
    update_step = new_first / corr_one / (jnp.sqrt(new_second / corr_two) + adam_eps)
    updated = (old_rows.astype(jnp.float32) - learn_rate * update_step).astype(jnp.bfloat16)
    return (new_first, new_second, updated)


def long_way(picks, pick_weights, token_grads, values, first_moment, second_moment, projectors):
    mem = ("y", "z", "c")
    owners = lax.axis_size(mem)
    rows_dev = values.shape[0]
    width = values.shape[1]
    tok_count, per_token = picks.shape
    proj_count = projectors.shape[0]
    out_width = projectors.shape[2]
    total_picks = tok_count * per_token
    capacity = 2 * total_picks // owners
    flat_picks = picks.reshape(-1)
    owner_ids = flat_picks // rows_dev
    local_rows = flat_picks - owner_ids * rows_dev
    member = (owner_ids[:, None] == jnp.arange(owners, dtype=jnp.int32)[None, :]).astype(jnp.int32)
    before = jnp.cumsum(member, axis=0) - member
    slot_ids = owner_ids * capacity + jnp.sum(before * member, axis=1)
    proj_ids = picks % proj_count
    flat_proj = projectors.reshape(proj_count * width, out_width)
    requests = jnp.zeros((owners * capacity,), jnp.int32).at[slot_ids].set(local_rows)
    requests = requests.reshape(owners, capacity)
    received = lax.all_to_all(requests, mem, split_axis=0, concat_axis=0, tiled=True)
    looked = values[received]
    returned = lax.all_to_all(looked, mem, split_axis=0, concat_axis=0, tiled=True)
    back_grads = lax.dot_general(token_grads, flat_proj, NT, preferred_element_type=jnp.float32)
    back_grads = back_grads.astype(jnp.bfloat16).reshape(tok_count, proj_count, width)
    chosen = back_grads[jnp.arange(tok_count, dtype=jnp.int32)[:, None], proj_ids].reshape(
        total_picks, width
    )
    grad_rows = jnp.zeros((owners * capacity, width), jnp.bfloat16).at[slot_ids].set(chosen)
    grad_wts = (
        jnp.zeros((owners * capacity,), jnp.bfloat16).at[slot_ids].set(pick_weights.reshape(-1))
    )
    got_rows = lax.all_to_all(
        grad_rows.reshape(owners, capacity, width), mem, split_axis=0, concat_axis=0, tiled=True
    )
    got_wts = lax.all_to_all(
        grad_wts.reshape(owners, capacity), mem, split_axis=0, concat_axis=0, tiled=True
    )
    picked = returned.reshape(owners * capacity, width)[slot_ids].reshape(
        tok_count, per_token, width
    )
    mixing = jnp.where(
        proj_ids[..., None] == jnp.arange(proj_count, dtype=jnp.int32),
        pick_weights[..., None],
        jnp.zeros((), jnp.bfloat16),
    )
    proj_sums = jnp.einsum(
        "tjp,tjd->tpd", mixing, picked, preferred_element_type=jnp.float32
    ).astype(jnp.bfloat16)
    layer_out = jnp.dot(
        proj_sums.reshape(tok_count, proj_count * width),
        flat_proj,
        preferred_element_type=jnp.float32,
    ).astype(jnp.bfloat16)
    weighted = got_wts.astype(jnp.float32)[..., None] * got_rows.astype(jnp.float32)
    slab_grad = (
        jnp.zeros((rows_dev, width), jnp.float32)
        .at[received.reshape(-1)]
        .add(weighted.reshape(-1, width))
    )
    quarter = first_moment.shape[0]
    start = lax.axis_index("x") * quarter
    share = lax.psum_scatter(slab_grad, "x", scatter_dimension=0, tiled=True)
    old_rows = lax.dynamic_slice_in_dim(values, start, quarter, 0)
    new_first, new_second, new_part = adam_rows(old_rows, share, first_moment, second_moment)
    new_values = lax.all_gather(new_part, "x", axis=0, tiled=True)
    return (layer_out, new_values, new_first, new_second)


def call(kernel, out_shape, grid=None, in_specs=None, out_specs=None, scratch=(), cost=None):
    extra = {} if grid is None else {"grid": grid}
    if in_specs is not None:
        extra["in_specs"] = in_specs
    if out_specs is not None:
        extra["out_specs"] = out_specs
    return pl.pallas_call(
        kernel,
        out_shape=out_shape,
        scratch_shapes=list(scratch),
        compiler_params=pltpu.CompilerParams(vmem_limit_bytes=VMEM),
        cost_estimate=cost,
        **extra,
    )


def cost(flops, nbytes):
    return pl.CostEstimate(flops=flops, bytes_accessed=nbytes, transcendentals=0)


def rank_kernel(cells, block, cell_ref, trow_ref, rank_ref, req_ref):
    count = cell_ref.shape[1]
    below = lax.broadcasted_iota(jnp.int32, (block, block), 0) < lax.broadcasted_iota(
        jnp.int32, (block, block), 1
    )
    below = below.astype(F32).astype(BF)
    carry = jnp.zeros((cells, 1), F32)
    asked = jnp.zeros((3 * cells, LANES), F32)
    for b in range(count // block):
        span = pl.ds(b * block, block)
        cell = cell_ref[:, span]
        trow = trow_ref[:, span]
        here = (lax.broadcasted_iota(jnp.int32, (cells, block), 0) == cell).astype(F32)
        before = jnp.dot(here.astype(BF), below, preferred_element_type=F32) + carry
        carry = carry + jnp.sum(here, axis=1, keepdims=True)
        rank = jnp.sum(here * before, axis=0, keepdims=True).astype(jnp.int32)
        rank_ref[:, span] = rank
        place = (lax.broadcasted_iota(jnp.int32, (LANES, block), 0) == rank).astype(F32)
        high = (trow >> 5).astype(F32)
        low = (trow & 31).astype(F32)
        told = jnp.concatenate([here, here * high, here * low], axis=0)
        asked = asked + lax.dot_general(
            told.astype(BF), place.astype(BF), NT, preferred_element_type=F32
        )
    there = asked[:cells]
    rows = (asked[cells : 2 * cells] * 32.0 + asked[2 * cells :]).astype(jnp.int32)
    rows = jnp.where(there > 0.5, rows, -1)
    lane = lax.broadcasted_iota(jnp.int32, (cells, LANES), 1)
    over = (jnp.max(carry) > CAP).astype(jnp.int32)
    req_ref[...] = jnp.where(lane == LANES - 1, over, rows)


def send_kernel(
    cells, tok, tg_ref, proj_ref, pcol_ref, cell_ref, rank_ref, wt_ref, out_ref, chosen, place
):
    step = pl.program_id(0)
    per_token = pcol_ref.shape[1]
    back = lax.dot_general(tg_ref[...], proj_ref[0], NT, preferred_element_type=F32)
    back = back.astype(BF)
    for j in range(per_token):
        mine = pcol_ref[:, j : j + 1] == step
        span = pl.ds(j * tok, tok)

        @pl.when(step == 0)
        def _():
            chosen[span, :] = back

        @pl.when(step > 0)
        def _():
            chosen[span, :] = jnp.where(mine, back, chosen[span, :])

    @pl.when(step == pl.num_programs(0) - 1)
    def _():
        count = cell_ref.shape[1]
        at = lax.broadcasted_iota(jnp.int32, (CAP, count), 0) == rank_ref[...]
        place[...] = jnp.where(at, wt_ref[...].astype(F32), 0.0).astype(BF)
        group = 4
        for g in range(cells // group):
            parts = []
            for d in range(g * group, (g + 1) * group):
                here = (cell_ref[...] == d).astype(F32).astype(BF)
                parts.append(place[...] * here)
            pick = jnp.concatenate(parts, axis=0)
            out_ref[pl.ds(g * group * CAP, group * CAP), :] = jnp.dot(
                pick, chosen[...], preferred_element_type=F32
            ).astype(BF)


def look_kernel(ids_ref, table_ref, out_ref):
    rows = ids_ref.shape[0]
    total = table_ref.shape[0]
    pick = lax.broadcasted_iota(jnp.int32, (rows, total), 1) == ids_ref[...]
    out_ref[...] = jnp.dot(
        pick.astype(F32).astype(BF), table_ref[...], preferred_element_type=F32
    ).astype(BF)


def sum_kernel(rows, ids_ref, flags_ref, got_ref, out_ref):
    base = pl.program_id(0) * rows
    slots = ids_ref.shape[1]
    pick = lax.broadcasted_iota(jnp.int32, (rows, slots), 0) + base == ids_ref[...]
    out_ref[:rows, :] = jnp.dot(
        pick.astype(F32).astype(BF), got_ref[...], preferred_element_type=F32
    ).astype(out_ref.dtype)
    over = jnp.max(flags_ref[...]).astype(F32)
    out_ref[rows:, :] = jnp.full((FLAG_ROWS, out_ref.shape[1]), over, F32).astype(out_ref.dtype)


def out_kernel(slot_ref, pcol_ref, wcol_ref, ret_ref, proj_ref, out_ref, picked, total):
    step = pl.program_id(0)
    tok, per_token = slot_ref.shape
    slots = ret_ref.shape[0]

    @pl.when(step == 0)
    def _():
        lane = lax.broadcasted_iota(jnp.int32, (tok, slots), 1)
        for j in range(per_token):
            pick = (lane == slot_ref[:, j : j + 1]).astype(F32).astype(BF)
            row = jnp.dot(pick, ret_ref[...], preferred_element_type=F32)
            picked[j] = row * wcol_ref[:, j : j + 1]

    sums = jnp.zeros(picked.shape[1:], F32)
    for j in range(per_token):
        sums = sums + jnp.where(pcol_ref[:, j : j + 1] == step, picked[j], 0.0)
    part = jnp.dot(sums.astype(BF), proj_ref[0], preferred_element_type=F32)

    @pl.when(step == 0)
    def _():
        total[...] = part

    @pl.when(step > 0)
    def _():
        total[...] += part

    @pl.when(step == pl.num_programs(0) - 1)
    def _():
        out_ref[...] = total[...].astype(BF)


def short_way(picks, pick_weights, token_grads, values, first_moment, second_moment, projectors):
    plane = ("y", "c", "x")
    cells = lax.axis_size(plane)
    depth = lax.axis_size("z")
    parts = lax.axis_size("x")
    rows_dev, width = values.shape
    quarter = rows_dev // parts
    tok, per_token = picks.shape
    proj_count, _, out_width = projectors.shape
    total = tok * per_token
    slots = cells * CAP
    table_rows = depth * quarter
    start = lax.axis_index("x") * quarter
    old_rows = lax.dynamic_slice_in_dim(values, start, quarter, 0)
    table = lax.all_gather(old_rows, "z", axis=0, tiled=True)

    by_pick = picks.T.reshape(1, total)
    owner = by_pick // rows_dev
    row = by_pick % rows_dev
    owner_y = owner // (depth * CORES)
    owner_z = (owner // CORES) % depth
    cell = (owner_y * CORES + owner % CORES) * parts + row // quarter
    trow = owner_z * quarter + row % quarter
    block = 256
    rank, requests = call(
        functools.partial(rank_kernel, cells, block),
        (
            jax.ShapeDtypeStruct((1, total), jnp.int32),
            jax.ShapeDtypeStruct((cells, LANES), jnp.int32),
        ),
        cost=cost(2 * total * cells * 400, 20000),
    )(cell, trow)
    received = lax.all_to_all(requests, plane, split_axis=0, concat_axis=0, tiled=True)

    pcol = picks % proj_count
    wt_row = pick_weights.T.reshape(1, total)
    whole = lambda shape: pl.BlockSpec(shape, lambda i: (0,) * len(shape))
    sent = call(
        functools.partial(send_kernel, cells, tok),
        jax.ShapeDtypeStruct((slots, width), BF),
        grid=(proj_count,),
        in_specs=[
            whole((tok, out_width)),
            pl.BlockSpec((1, width, out_width), lambda i: (i, 0, 0)),
            whole((tok, per_token)),
            whole((1, total)),
            whole((1, total)),
            whole((1, total)),
        ],
        out_specs=whole((slots, width)),
        scratch=[pltpu.VMEM((total, width), BF), pltpu.VMEM((CAP, total), BF)],
        cost=cost(2 * width * (tok * proj_count * out_width + slots * total), 12000000),
    )(token_grads, projectors, pcol, cell, rank, wt_row)
    got = lax.all_to_all(
        sent.reshape(cells, CAP, width), plane, split_axis=0, concat_axis=0, tiled=True
    ).reshape(slots, width)

    asked = received[:, :CAP]
    flags = received[:, LANES - 1 :]
    chunk = slots // 8
    looked = call(
        look_kernel,
        jax.ShapeDtypeStruct((slots, width), BF),
        grid=(8,),
        in_specs=[
            pl.BlockSpec((chunk, 1), lambda i: (i, 0)),
            whole((table_rows, width)),
        ],
        out_specs=pl.BlockSpec((chunk, width), lambda i: (i, 0)),
        cost=cost(2 * width * slots * table_rows, 4000000),
    )(asked.reshape(slots, 1), table)
    returned = lax.all_to_all(
        looked.reshape(cells, CAP, width), plane, split_axis=0, concat_axis=0, tiled=True
    ).reshape(slots, width)

    sums = call(
        functools.partial(sum_kernel, quarter),
        jax.ShapeDtypeStruct((depth * (quarter + FLAG_ROWS), width), BF),
        grid=(depth,),
        in_specs=[whole((1, slots)), whole((cells, 1)), whole((slots, width))],
        out_specs=pl.BlockSpec((quarter + FLAG_ROWS, width), lambda i: (i, 0)),
        cost=cost(2 * width * slots * table_rows, 4000000),
    )(asked.reshape(1, slots), flags, got)
    share = lax.psum_scatter(sums, "z", scatter_dimension=0, tiled=True).astype(F32)
    flag = share[quarter, 0]
    new_first, new_second, new_part = adam_rows(
        old_rows, share[:quarter], first_moment, second_moment
    )
    new_values = lax.all_gather(new_part, "x", axis=0, tiled=True)

    slot_col = (cell * CAP + rank).reshape(per_token, tok).T
    layer_out = call(
        out_kernel,
        jax.ShapeDtypeStruct((tok, out_width), BF),
        grid=(proj_count,),
        in_specs=[
            whole((tok, per_token)),
            whole((tok, per_token)),
            whole((tok, per_token)),
            whole((slots, width)),
            pl.BlockSpec((1, width, out_width), lambda i: (i, 0, 0)),
        ],
        out_specs=whole((tok, out_width)),
        scratch=[
            pltpu.VMEM((per_token, tok, width), F32),
            pltpu.VMEM((tok, out_width), F32),
        ],
        cost=cost(2 * width * (tok * proj_count * out_width + slots * total), 13000000),
    )(slot_col, pcol, pick_weights.astype(F32), returned, projectors)
    return flag, (layer_out, new_values, new_first, new_second)


def on_device(*args):
    flag, outs = short_way(*args)
    return lax.cond(flag > 0.5, lambda given, done: long_way(*given), lambda given, done: done, args, outs)


def solution(mesh):
    mem, dp = mesh.devices.shape
    grid = Mesh(
        mesh.devices.reshape(mem // (Z_CHIPS * CORES), Z_CHIPS, CORES, dp), ("y", "z", "c", "x")
    )
    every = P(("y", "z", "c", "x"), None)
    slab = P(("y", "z", "c"), None)
    return jax.shard_map(
        on_device,
        mesh=grid,
        in_specs=(every, every, every, slab, every, every, P()),
        out_specs=(every, slab, every, every),
        check_vma=False,
    )
```

time: 282 us -> 245 us (0.87)
  local copies, waits for them, and re-layouts: 63.6 us -> 14.1 us
  Pallas kernels: 0 us -> 42.7 us
  other arithmetic: 43.7 us -> 5.37 us
  blocking collectives: 13.4 us -> 35.2 us
  starting transfers between devices: 40 us -> 22.6 us
  waiting for transfers between devices: 90.8 us -> 107 us
  matrix products: 15.8 us -> 0 us
    all_to_all x4 -> x3, waiting for transfers between devices: 90.8 us -> 31 us  [the longest x1 31 us: short_way(): lax.all_to_all(sent.reshape(cells, CAP, width), plane, split_axis=0, conc...]
    pallas_call x0 -> x5, Pallas kernels: none -> 42.7 us  [the longest x1 12.9 us: short_way(): call(out_kernel, jax.ShapeDtypeStruct((tok, out_width), BF), grid=(proj_c...]
    scatter x3 -> x0, local copies, waits for them, and re-layouts: 40.5 us -> none  [the longest x1 22.6 us: on_device(): jnp.zeros((owners * capacity, width), jnp.bfloat16).at[slot_ids].set(chosen)]
    reduce_scatter x1, waiting for transfers between devices: 0.01 us -> 39.8 us  [short_way(): lax.psum_scatter(sums, 'z', scatter_dimension=0, tiled=True).astype(F32)]
    all_gather x0 -> x1, waiting for transfers between devices: none -> 36.4 us  [short_way(): table = lax.all_gather(old_rows, 'z', axis=0, tiled=True)]
    all_gather x1, blocking collectives: 13.4 us -> 35.2 us  [short_way(): new_values = lax.all_gather(new_part, 'x', axis=0, tiled=True)]
    another operation x3 -> x0, other arithmetic: 18.4 us -> none
    scatter-add x1 -> x0, other arithmetic: 17.9 us -> none  [on_device(): slab_grad = jnp.zeros((rows_dev, width), jnp.float32).at[received.reshape...]
  transfers between devices with their start and end apart: 5 -> 5, of which waited for: 2 -> 3; matrix products, arithmetic and copies ran while one was open for 30% -> 4% of each run, Pallas kernels for 0% -> 5%
where the time goes in v1:
time: 245 us; the launch traced here: 243 us
  waiting for transfers between devices  107 us (44%)
  Pallas kernels  42.7 us (17%)
  blocking collectives  35.2 us (14%)
  starting transfers between devices  22.6 us (9%)
  between operations  14.8 us (6%)
  local copies, waits for them, and re-layouts  14.1 us (6%)
  other arithmetic  5.37 us (2%)
    reduce_scatter x1, waiting for transfers between devices, short_way(): lax.psum_scatter(sums, 'z', scatter_dimension=0, tiled=True).astype(F32)  39.8 us
    all_gather x1, waiting for transfers between devices, short_way(): table = lax.all_gather(old_rows, 'z', axis=0, tiled=True)  36.4 us
    all_gather x1, blocking collectives, short_way(): new_values = lax.all_gather(new_part, 'x', axis=0, tiled=True)  35.2 us
    all_to_all x1, waiting for transfers between devices, short_way(): lax.all_to_all(sent.reshape(cells, CAP, width), plane, split_axis=0, conc...  31 us
    pallas_call x1, Pallas kernels, short_way(): call(out_kernel, jax.ShapeDtypeStruct((tok, out_width), BF), grid=(proj_c...  12.9 us
    pallas_call x1, Pallas kernels, short_way(): call(functools.partial(send_kernel, cells, tok), jax.ShapeDtypeStruct((sl...  12.6 us
    pallas_call x1, Pallas kernels, short_way(): call(look_kernel, jax.ShapeDtypeStruct((slots, width), BF), grid=(8,), in...  8.38 us
    all_to_all x1, starting transfers between devices, short_way(): lax.all_to_all(requests, plane, split_axis=0, concat_axis=0, tiled=True)  7.62 us
  transfers between devices with their start and end apart: 5, of which 3 were waited for; matrix products, arithmetic and copies ran while one was open for 4% of the time, Pallas kernels for 5%

profile of v1, /device:TPU:2, one launch (start us, length us, event | category | flops | bytes accessed | tf_op | source)
XLA Modules:
  0.0 242.6 jit_solution(11057837460768004420)
XLA Ops:
  7.2 0.8 reshape.740
  7.9 0.7 fusion.36
  8.6 0.7 multiply_add_fusion.2.cell_ref
  9.3 1.8 shard_map.110
  11.1 7.6 %all-to-all-start.4 = ((s32[32,1,128]{2,1,0:T(1,128)}), s32[32,1,128]{2,1,0:T(1,128)S(1)}, u32[]{:S(2)}, u32[]{:S(2)}) async-start(s32[32,1,128]{2,1,0:T(1,128)} %bitcast.73), calls=%async_computation.5 | async-start | bytes 32768 | tf_op jit(solution)/shard_map/all_to_all | solution.py:277
  18.8 0.7 broadcast_compare_fusion
  19.5 0.8 copy.62
  20.3 0.2 copy.65
  20.5 1.4 reshape.742.wt_ref
  21.8 0.7 add_select_fusion.3.pcol_ref
  22.6 12.6 %shard_map.111 = bf16[2560,512]{1,0:T(8,128)(2,1)} custom-call(bf16[320,2048]{1,0:T(8,128)(2,1)} %tg_ref.1, bf16[4,512,2048]{2,1,0:T(8,128)(2,1)} %proj_ref.3, s32[320,4]{1,0:T(8,128)} %add_select_fusion.3.pcol_ref, s32[1,1280]{1,0:T(1,128)} %multiply_add_fusion.2.cell_ref, s32[1,1280]{1,0:T(1,128)} %get-tuple-element.36.rank_ref, ...), custom_call_target="tpu_custom_call" | custom-call | flops 6039797760 | bytes 12000000 | tf_op jit(solution)/shard_map/pallas_call | solution.py:282
  35.1 0.0 all-to-all-done.4
  35.1 7.4 %all-to-all-start.5 = ((bf16[32,80,512]{2,1,0:T(8,128)(2,1)}), bf16[32,80,512]{2,1,0:T(8,128)(2,1)S(1)}, u32[]{:S(2)}, u32[]{:S(2)}) async-start(bf16[32,80,512]{2,1,0:T(8,128)(2,1)} %bitcast.61), calls=%async_computation.6 | async-start | bytes 5242880 | tf_op jit(solution)/shard_map/all_to_all | solution.py:298
  42.5 0.0 reduce-scatter.5.cloned.1.call-start
  42.6 0.7 slice.31.flags_ref
  43.3 0.7 reshape.741.ids_ref
  43.9 31.0 %all-to-all-done.5 = bf16[32,80,512]{2,1,0:T(8,128)(2,1)S(1)} async-done(((bf16[32,80,512]{2,1,0:T(8,128)(2,1)}), bf16[32,80,512]{2,1,0:T(8,128)(2,1)S(1)}, u32[]{:S(2)}, u32[]{:S(2)}) %all-to-all-start.5) | async-done | bytes 2621472 | tf_op jit(solution)/shard_map/all_to_all | solution.py:298
  75.0 1.5 copy-done.3
  76.5 7.1 %shard_map.112 = bf16[1152,512]{1,0:T(8,128)(2,1)} custom-call(s32[1,2560]{1,0:T(1,128)} %reshape.741.ids_ref, s32[32,1]{1,0:T(8,128)} %slice.31.flags_ref, bf16[2560,512]{1,0:T(8,128)(2,1)} %bitcast.62), custom_call_target="tpu_custom_call" | custom-call | flops 2684354560 | bytes 4000000 | tf_op jit(solution)/shard_map/pallas_call | solution.py:320
  83.6 0.0 reduce-scatter.5.cloned.1.call-update
  83.6 0.0 all-gather.2.cloned.1.call-start
  83.7 39.8 %reduce-scatter.5.cloned.1.call-done = bf16[144,512]{1,0:T(8,128)(2,1)} async-done(((bf16[1152,512]{1,0:T(8,128)(2,1)}), bf16[144,512]{1,0:T(8,128)(2,1)}) %reduce-scatter.5.cloned.1.call-update) | async-done | bytes 147472 | tf_op jit(solution)/shard_map/reduce_scatter | solution.py:328
  123.5 0.9 convert_element_type.53
  124.4 0.0 copy-done
  124.4 0.0 copy-done.4
  124.4 0.0 copy-done.6
  124.4 0.9 subtract_convert_fusion.1
  125.4 0.0 all-gather.2.cloned.1.call-update
  125.4 1.7 reshape.813.ids_ref
  127.1 36.4 %all-gather.2.cloned.1.call-done.table_ref = bf16[1024,512]{1,0:T(8,128)(2,1)} async-done(((bf16[128,512]{1,0:T(8,128)(2,1)}), bf16[1024,512]{1,0:T(8,128)(2,1)}) %all-gather.2.cloned.1.call-update) | async-done | bytes 1048592 | tf_op jit(solution)/shard_map/all_gather | solution.py:259
  163.5 8.4 %shard_map.113 = bf16[2560,512]{1,0:T(8,128)(2,1)} custom-call(s32[2560,1]{1,0:T(8,128)} %reshape.813.ids_ref, bf16[1024,512]{1,0:T(8,128)(2,1)} %all-gather.2.cloned.1.call-done.table_ref), custom_call_target="tpu_custom_call" | custom-call | flops 2684354560 | bytes 4000000 | tf_op jit(solution)/shard_map/pallas_call | solution.py:305
  171.9 7.5 %all-to-all-start.6 = ((bf16[32,80,512]{2,1,0:T(8,128)(2,1)}), bf16[32,80,512]{2,1,0:T(8,128)(2,1)S(1)}, u32[]{:S(2)}, u32[]{:S(2)}) async-start(bf16[32,80,512]{2,1,0:T(8,128)(2,1)} %bitcast.60), calls=%async_computation.8 | async-start | bytes 5242880 | tf_op jit(solution)/shard_map/all_to_all | solution.py:316
  179.4 0.0 copy-done.14
  179.4 0.8 copy.68.wcol_ref
  180.2 0.0 copy-done.16
  180.2 0.7 add_reduce_fusion
  181.0 0.1 reshape.745
  181.0 0.8 copy.66
  181.9 1.2 slice.32
  183.7 35.2 %all_gather.10 = bf16[512,512]{1,0:T(8,128)(2,1)} all-gather(bf16[128,512]{1,0:T(8,128)(2,1)S(1)} %get-tuple-element.76), channel_id=1, replica_groups=mesh['y'=4,'z'=8,'c'=2,'x'=4] {'x'}, dimensions={0}, use_global_device_ids=true | all-gather | bytes 655360 | tf_op jit(solution)/shard_map/all_gather | solution.py:333
  218.9 0.0 all-to-all-done.6
  218.9 1.5 copy-done.2
  220.4 12.9 %shard_map.114 = bf16[320,2048]{1,0:T(8,128)(2,1)} custom-call(s32[320,4]{1,0:T(8,128)} %bitcast.67, s32[320,4]{1,0:T(8,128)} %add_select_fusion.3.pcol_ref, f32[320,4]{1,0:T(8,128)} %copy.68.wcol_ref, bf16[2560,512]{1,0:T(8,128)(2,1)} %bitcast.59, bf16[4,512,2048]{2,1,0:T(8,128)(2,1)} %proj_ref.3), custom_call_target="tpu_custom_call" | custom-call | flops 6039797760 | bytes 13000000 | tf_op jit(solution)/shard_map/pallas_call | solution.py:336
  233.3 0.0 copy-done.15
  233.3 0.4 conditional.1
  233.8 0.0 copy-start.8
  233.8 2.0 copy.86
  235.7 0.0 copy-done.8
  (10 shorter events, 0.0 us)
Async XLA Ops:
  11.1 24.0 %all-to-all-start.4 = ((s32[32,1,128]{2,1,0:T(1,128)}), s32[32,1,128]{2,1,0:T(1,128)S(1)}, u32[]{:S(2)}, u32[]{:S(2)}) async-start(s32[32,1,128]{2,1,0:T(1,128)} %bitcast.73), calls=%async_computation.5 | async-start | bytes 32768 | tf_op jit(solution)/shard_map/all_to_all | solution.py:277
  35.1 39.8 %all-to-all-start.5 = ((bf16[32,80,512]{2,1,0:T(8,128)(2,1)}), bf16[32,80,512]{2,1,0:T(8,128)(2,1)S(1)}, u32[]{:S(2)}, u32[]{:S(2)}) async-start(bf16[32,80,512]{2,1,0:T(8,128)(2,1)} %bitcast.61), calls=%async_computation.6 | async-start | bytes 5242880 | tf_op jit(solution)/shard_map/all_to_all | solution.py:298
  42.5 80.9 %reduce-scatter.5.cloned.1.call-start = ((), (), s32[]{:S(2)}) async-start(), calls=%async_computation.10 | async-start | bytes 1327104 | tf_op jit(solution)/shard_map/reduce_scatter | solution.py:328
  75.0 1.5 copy-start.3
  83.6 40.8 %copy-start = (bf16[512,512]{1,0:T(8,128)(2,1)S(1)}, bf16[512,512]{1,0:T(8,128)(2,1)}, u32[]{:S(2)}) copy-start(bf16[512,512]{1,0:T(8,128)(2,1)} %param.12) | copy-start | bytes 1572868
  83.6 40.8 %copy-start.4 = (f32[128,512]{1,0:T(8,128)S(1)}, f32[128,512]{1,0:T(8,128)}, u32[]{:S(2)}) copy-start(f32[128,512]{1,0:T(8,128)} %param.13) | copy-start | bytes 786436
  83.6 40.8 %copy-start.6 = (f32[128,512]{1,0:T(8,128)S(1)}, f32[128,512]{1,0:T(8,128)}, u32[]{:S(2)}) copy-start(f32[128,512]{1,0:T(8,128)} %param.14) | copy-start | bytes 786436
  83.6 79.9 %all-gather.2.cloned.1.call-start = ((), (), s32[]{:S(2)}) async-start(), calls=%async_computation.11 | async-start | bytes 1179648 | tf_op jit(solution)/shard_map/all_gather | solution.py:259
  171.9 7.6 %copy-start.14 = (bf16[320,4]{0,1:T(4,128)(2,1)S(1)}, bf16[320,4]{0,1:T(4,128)(2,1)}, u32[]{:S(2)}) copy-start(bf16[320,4]{0,1:T(4,128)(2,1)} %param.10) | copy-start | bytes 7684
  171.9 8.4 %copy-start.16 = (s32[1,1280]{1,0:T(1,128)S(1)}, s32[1,1280]{1,0:T(1,128)}, u32[]{:S(2)}) copy-start(s32[1,1280]{1,0:T(1,128)} %multiply_add_fusion.2.cell_ref) | copy-start | bytes 15364
  171.9 47.0 %all-to-all-start.6 = ((bf16[32,80,512]{2,1,0:T(8,128)(2,1)}), bf16[32,80,512]{2,1,0:T(8,128)(2,1)S(1)}, u32[]{:S(2)}, u32[]{:S(2)}) async-start(bf16[32,80,512]{2,1,0:T(8,128)(2,1)} %bitcast.60), calls=%async_computation.8 | async-start | bytes 5242880 | tf_op jit(solution)/shard_map/all_to_all | solution.py:316
  218.9 1.5 copy-start.2
  220.4 12.9 %copy-start.11 = (s32[320,4]{0,1:T(4,128)S(1)}, s32[320,4]{0,1:T(4,128)}, u32[]{:S(2)}) copy-start(s32[320,4]{0,1:T(4,128)} %param.9) | copy-start | bytes 15364
  220.4 12.9 %copy-start.15 = (bf16[320,4]{0,1:T(4,128)(2,1)S(1)}, bf16[320,4]{0,1:T(4,128)(2,1)}, u32[]{:S(2)}) copy-start(bf16[320,4]{0,1:T(4,128)(2,1)} %param.10) | copy-start | bytes 7684
  233.8 2.0 copy-start.8
Sparse Core Ops, SparseCore 0:
  83.7 39.6 reduce-scatter.4
  126.0 37.4 all-gather.1

commit v2 on v1

--- a/solution.py
+++ b/solution.py
@@ -20,7 +20,7 @@
 CAP = 80
 LANES = 128
 FLAG_ROWS = 16
-VMEM = 56 * 1024 * 1024
+VMEM = 40 * 1024 * 1024
 BF = jnp.bfloat16
 F32 = jnp.float32
 NT = (((1,), (1,)), ((), ()))
@@ -200,15 +200,20 @@
     ).astype(BF)
 
 
-def sum_kernel(rows, ids_ref, flags_ref, got_ref, out_ref):
-    base = pl.program_id(0) * rows
+def sum_kernel(ids_ref, flags_ref, z_ref, got_ref, *out_refs):
+    depth = len(out_refs)
+    rows = out_refs[0].shape[0] - FLAG_ROWS
     slots = ids_ref.shape[1]
-    pick = lax.broadcasted_iota(jnp.int32, (rows, slots), 0) + base == ids_ref[...]
-    out_ref[:rows, :] = jnp.dot(
-        pick.astype(F32).astype(BF), got_ref[...], preferred_element_type=F32
-    ).astype(out_ref.dtype)
     over = jnp.max(flags_ref[...]).astype(F32)
-    out_ref[rows:, :] = jnp.full((FLAG_ROWS, out_ref.shape[1]), over, F32).astype(out_ref.dtype)
+    for k, out_ref in enumerate(out_refs):
+        base = lax.rem(z_ref[0] + k, depth) * rows
+        pick = lax.broadcasted_iota(jnp.int32, (rows, slots), 0) == ids_ref[...] - base
+        out_ref[:rows, :] = jnp.dot(
+            pick.astype(F32).astype(BF), got_ref[...], preferred_element_type=F32
+        ).astype(out_ref.dtype)
+        out_ref[rows:, :] = jnp.full((FLAG_ROWS, out_ref.shape[1]), over, F32).astype(
+            out_ref.dtype
+        )
 
 
 def out_kernel(slot_ref, pcol_ref, wcol_ref, ret_ref, proj_ref, out_ref, picked, total):
@@ -301,6 +306,7 @@
 
     asked = received[:, :CAP]
     flags = received[:, LANES - 1 :]
+    vmem = pl.BlockSpec(memory_space=pltpu.VMEM)
     chunk = slots // 8
     looked = call(
         look_kernel,
@@ -313,24 +319,37 @@
         out_specs=pl.BlockSpec((chunk, width), lambda i: (i, 0)),
         cost=cost(2 * width * slots * table_rows, 4000000),
     )(asked.reshape(slots, 1), table)
+    got, looked = lax.optimization_barrier((got, looked))
     returned = lax.all_to_all(
         looked.reshape(cells, CAP, width), plane, split_axis=0, concat_axis=0, tiled=True
     ).reshape(slots, width)
 
+    z_here = lax.axis_index("z").reshape(1)
     sums = call(
-        functools.partial(sum_kernel, quarter),
-        jax.ShapeDtypeStruct((depth * (quarter + FLAG_ROWS), width), BF),
-        grid=(depth,),
-        in_specs=[whole((1, slots)), whole((cells, 1)), whole((slots, width))],
-        out_specs=pl.BlockSpec((quarter + FLAG_ROWS, width), lambda i: (i, 0)),
+        sum_kernel,
+        (jax.ShapeDtypeStruct((quarter + FLAG_ROWS, width), BF),) * depth,
+        in_specs=[vmem, vmem, pl.BlockSpec(memory_space=pltpu.SMEM), vmem],
+        out_specs=(vmem,) * depth,
         cost=cost(2 * width * slots * table_rows, 4000000),
-    )(asked.reshape(1, slots), flags, got)
-    share = lax.psum_scatter(sums, "z", scatter_dimension=0, tiled=True).astype(F32)
+    )(asked.reshape(1, slots), flags, z_here, got)
+    shares = [sums[0]] + [
+        lax.ppermute(sums[k], "z", [(i, (i + k) % depth) for i in range(depth)])
+        for k in range(1, depth)
+    ]
+    share = functools.reduce(lambda p, q: p + q, [s.astype(F32) for s in shares])
     flag = share[quarter, 0]
     new_first, new_second, new_part = adam_rows(
         old_rows, share[:quarter], first_moment, second_moment
     )
-    new_values = lax.all_gather(new_part, "x", axis=0, tiled=True)
+    x_here = lax.axis_index("x")
+    new_values = jnp.zeros((parts, quarter, width), BF)
+    for k in range(parts):
+        piece = new_part
+        if k:
+            piece = lax.ppermute(new_part, "x", [(i, (i + k) % parts) for i in range(parts)])
+        mine = jnp.arange(parts) == (x_here - k) % parts
+        new_values = jnp.where(mine[:, None, None], piece[None], new_values)
+    new_values = new_values.reshape(rows_dev, width)
 
     slot_col = (cell * CAP + rank).reshape(per_token, tok).T
     layer_out = call(

time: 245 us -> 174 us (0.71)
  waiting for transfers between devices: 107 us -> 60.4 us
  blocking collectives: 35.2 us -> 0 us
  starting transfers between devices: 22.6 us -> 40.8 us
  Pallas kernels: 42.7 us -> 33.6 us
  local copies, waits for them, and re-layouts: 14.1 us -> 17.9 us
    reduce_scatter x1 -> x0, waiting for transfers between devices: 39.8 us -> none  [short_way(): lax.psum_scatter(sums, 'z', scatter_dimension=0, tiled=True).astype(F32)]
    all_gather x1 -> x0, blocking collectives: 35.2 us -> none  [short_way(): new_values = lax.all_gather(new_part, 'x', axis=0, tiled=True)]
    all_to_all x1, waiting for transfers between devices: 31 us -> 0.01 us  [short_way(): lax.all_to_all(sent.reshape(cells, CAP, width), plane, split_axis=0, conc...]
    ppermute x0 -> x10, waiting for transfers between devices: none -> 19 us  [the longest x7 19 us: short_way(): lax.ppermute(sums[k], 'z', [(i, (i + k) % depth) for i in range(depth)])]
    ppermute x0 -> x10, starting transfers between devices: none -> 18.3 us  [the longest x7 13.6 us: short_way(): lax.ppermute(sums[k], 'z', [(i, (i + k) % depth) for i in range(depth)])]
    all_gather x1, waiting for transfers between devices: 36.4 us -> 41.3 us  [short_way(): table = lax.all_gather(old_rows, 'z', axis=0, tiled=True)]
    unnamed x22 -> x24, local copies, waits for them, and re-layouts: 5.84 us -> 9.66 us
    pallas_call x1, Pallas kernels: 7.08 us -> 3.5 us  [short_way(): call(sum_kernel, (jax.ShapeDtypeStruct((quarter + FLAG_ROWS, width), BF),...]
  transfers between devices with their start and end apart: 5 -> 14, of which waited for: 3 -> 6; matrix products, arithmetic and copies ran while one was open for 4% -> 7% of each run, Pallas kernels for 5% -> 19%
where the time goes in v2:
time: 174 us; the launch traced here: 173 us
  waiting for transfers between devices  60.4 us (35%)
  starting transfers between devices  40.8 us (23%)
  Pallas kernels  33.6 us (19%)
  local copies, waits for them, and re-layouts  17.9 us (10%)
  between operations  14.9 us (9%)
  other arithmetic  5.6 us (3%)
    all_gather x1, waiting for transfers between devices, short_way(): table = lax.all_gather(old_rows, 'z', axis=0, tiled=True)  41.3 us
    ppermute x7, waiting for transfers between devices, short_way(): lax.ppermute(sums[k], 'z', [(i, (i + k) % depth) for i in range(depth)])  19 us
    ppermute x7, starting transfers between devices, short_way(): lax.ppermute(sums[k], 'z', [(i, (i + k) % depth) for i in range(depth)])  13.6 us
    pallas_call x1, Pallas kernels, short_way(): call(out_kernel, jax.ShapeDtypeStruct((tok, out_width), BF), grid=(proj_c...  11.9 us
    pallas_call x1, Pallas kernels, short_way(): call(functools.partial(send_kernel, cells, tok), jax.ShapeDtypeStruct((sl...  11 us
    unnamed x24, local copies, waits for them, and re-layouts  9.66 us
    all_to_all x1, starting transfers between devices, short_way(): lax.all_to_all(requests, plane, split_axis=0, concat_axis=0, tiled=True)  7.62 us
    all_to_all x1, starting transfers between devices, short_way(): lax.all_to_all(looked.reshape(cells, CAP, width), plane, split_axis=0, co...  7.41 us
  transfers between devices with their start and end apart: 14, of which 6 were waited for; matrix products, arithmetic and copies ran while one was open for 7% of the time, Pallas kernels for 19%

profile of v2, /device:TPU:2, one launch (start us, length us, event | category | flops | bytes accessed | tf_op | source)
XLA Modules:
  0.0 173.5 jit_solution(10169056578514380304)
XLA Ops:
  7.2 0.8 reshape.768
  7.9 0.1 fusion.39
  8.1 1.1 shard_map.104
  9.2 7.6 %all-to-all-start.4 = ((s32[32,1,128]{2,1,0:T(1,128)}), s32[32,1,128]{2,1,0:T(1,128)S(1)}, u32[]{:S(2)}, u32[]{:S(2)}) async-start(s32[32,1,128]{2,1,0:T(1,128)} %bitcast.26), calls=%async_computation.5 | async-start | bytes 32768 | tf_op jit(solution)/shard_map/all_to_all | solution.py:282
  16.9 0.7 broadcast_compare_fusion
  17.6 0.8 copy.57
  18.4 0.2 copy.60
  18.6 0.8 reshape.771.wt_ref
  19.4 11.0 %shard_map.105 = bf16[2560,512]{1,0:T(8,128)(2,1)S(1)} custom-call(bf16[320,2048]{1,0:T(8,128)(2,1)} %tg_ref.1, bf16[4,512,2048]{2,1,0:T(8,128)(2,1)} %proj_ref.3, s32[320,4]{1,0:T(8,128)S(1)} %add_select_fusion.3.pcol_ref, s32[1,1280]{1,0:T(1,128)S(1)} %multiply_add_fusion.2.cell_ref, s32[1,1280]{1,0:T(1,128)S(1)} %get-tuple-element.217.rank_ref, ...), custom_call_target="tpu_custom_call" | custom-call | flops 6039797760 | bytes 12000000 | tf_op jit(solution)/shard_map/pallas_call | solution.py:287
  30.4 1.5 copy-done.2
  32.0 7.4 %all-to-all-start.5 = ((bf16[32,80,512]{2,1,0:T(8,128)(2,1)}), bf16[32,80,512]{2,1,0:T(8,128)(2,1)S(1)}, u32[]{:S(2)}, u32[]{:S(2)}) async-start(bf16[32,80,512]{2,1,0:T(8,128)(2,1)} %bitcast.89), calls=%async_computation.6 | async-start | bytes 5242880 | tf_op jit(solution)/shard_map/all_to_all | solution.py:303
  39.4 1.6 constant_dynamic-slice_fusion
  41.0 1.7 reshape.842.ids_ref
  42.7 41.3 %all-gather.2.cloned.1.call-done.table_ref = bf16[1024,512]{1,0:T(8,128)(2,1)} async-done(((bf16[128,512]{1,0:T(8,128)(2,1)}), bf16[1024,512]{1,0:T(8,128)(2,1)}) %all-gather.2.cloned.1.call-update) | async-done | bytes 1048592 | tf_op jit(solution)/shard_map/all_gather | solution.py:264
  84.0 1.3 copy-done.3
  85.3 1.2 copy-done.4
  86.5 6.1 %shard_map.106 = bf16[2560,512]{1,0:T(8,128)(2,1)} custom-call(s32[2560,1]{1,0:T(8,128)S(1)} %copy-done.3, bf16[1024,512]{1,0:T(8,128)(2,1)S(1)} %copy-done.4), custom_call_target="tpu_custom_call" | custom-call | flops 2684354560 | bytes 4000000 | tf_op jit(solution)/shard_map/pallas_call | solution.py:311
  92.6 1.5 copy-done
  94.1 7.4 %all-to-all-start.6 = ((bf16[32,80,512]{2,1,0:T(8,128)(2,1)}), bf16[32,80,512]{2,1,0:T(8,128)(2,1)S(1)}, u32[]{:S(2)}, u32[]{:S(2)}) async-start(bf16[32,80,512]{2,1,0:T(8,128)(2,1)} %bitcast.34), calls=%async_computation.7 | async-start | bytes 5242880 | tf_op jit(solution)/shard_map/all_to_all | solution.py:323
  101.6 0.1 reshape.769.ids_ref
  101.7 1.7 %copy-done.1 = bf16[32,80,512]{2,1,0:T(8,128)(2,1)S(1)} copy-done((bf16[32,80,512]{2,1,0:T(8,128)(2,1)S(1)}, bf16[32,80,512]{2,1,0:T(8,128)(2,1)}, u32[]{:S(2)}) %copy-start.1) | copy-done | bytes 2621464
  103.5 3.5 %shard_map.107 = (bf16[144,512]{1,0:T(8,128)(2,1)S(1)}, bf16[144,512]{1,0:T(8,128)(2,1)S(1)}, bf16[144,512]{1,0:T(8,128)(2,1)S(1)}, bf16[144,512]{1,0:T(8,128)(2...) custom-call(s32[1,2560]{1,0:T(1,128)S(1)} %reshape.769.ids_ref, ...), custom_call_target="tpu_custom_call" | custom-call | flops 2684354560 | bytes 4000000 | tf_op jit(solution)/shard_map/pallas_call | solution.py:328
  107.0 1.6 collective-permute-start.6
  108.6 2.0 %collective-permute-start.5 = (bf16[144,512]{1,0:T(8,128)(2,1)S(1)}, bf16[144,512]{1,0:T(8,128)(2,1)S(1)}, u32[]{:S(2)}, u32[]{:S(2)}) collective-permute-start(bf16[144,512]{1,0:T(8,128)(2,1)S(1)} %get-tuple-element.225), channel_id=1, source_target_pairs={{0,48},{8,56},{16,0},{24,8},{32,16},{40,24},{48,32},{56,40},{1,49}... | collective-permute-start | bytes 442376 | tf_op jit(solution)/shard_map/ppermute | solution.py:336
  110.5 2.1 %collective-permute-start.4 = (bf16[144,512]{1,0:T(8,128)(2,1)}, bf16[144,512]{1,0:T(8,128)(2,1)}, u32[]{:S(2)}, u32[]{:S(2)}) collective-permute-start(bf16[144,512]{1,0:T(8,128)(2,1)} %get-tuple-element.224), channel_id=1, source_target_pairs={{0,40},{8,48},{16,56},{24,0},{32,8},{40,16},{48,24},{56,32},{1,41}... | collective-permute-start | bytes 442376 | tf_op jit(solution)/shard_map/ppermute | solution.py:336
  112.7 2.6 %collective-permute-start.3 = (bf16[144,512]{1,0:T(8,128)(2,1)}, bf16[144,512]{1,0:T(8,128)(2,1)}, u32[]{:S(2)}, u32[]{:S(2)}) collective-permute-start(bf16[144,512]{1,0:T(8,128)(2,1)} %get-tuple-element.223), channel_id=1, source_target_pairs={{0,32},{8,40},{16,48},{24,56},{32,0},{40,8},{48,16},{56,24},{1,33}... | collective-permute-start | bytes 442376 | tf_op jit(solution)/shard_map/ppermute | solution.py:336
  115.2 1.8 %collective-permute-start.2 = (bf16[144,512]{1,0:T(8,128)(2,1)}, bf16[144,512]{1,0:T(8,128)(2,1)}, u32[]{:S(2)}, u32[]{:S(2)}) collective-permute-start(bf16[144,512]{1,0:T(8,128)(2,1)} %get-tuple-element.222), channel_id=1, source_target_pairs={{0,24},{8,32},{16,40},{24,48},{32,56},{40,0},{48,8},{56,16},{1,25}... | collective-permute-start | bytes 442376 | tf_op jit(solution)/shard_map/ppermute | solution.py:336
  117.0 3.6 %collective-permute-start.1 = (bf16[144,512]{1,0:T(8,128)(2,1)S(1)}, bf16[144,512]{1,0:T(8,128)(2,1)}, u32[]{:S(2)}, u32[]{:S(2)}) collective-permute-start(bf16[144,512]{1,0:T(8,128)(2,1)S(1)} %get-tuple-element.221), channel_id=1, source_target_pairs={{0,16},{8,24},{16,32},{24,40},{32,48},{40,56},{48,0},{56,8},{1,17}... | collective-permute-start | bytes 442376 | tf_op jit(solution)/shard_map/ppermute | solution.py:336
  120.6 2.4 %collective-permute-done.5 = bf16[144,512]{1,0:T(8,128)(2,1)S(1)} collective-permute-done((bf16[144,512]{1,0:T(8,128)(2,1)S(1)}, bf16[144,512]{1,0:T(8,128)(2,1)S(1)}, u32[]{:S(2)}, u32[]{:S(2)}) %collective-permute-start.5) | collective-permute-done | bytes 147488 | tf_op jit(solution)/shard_map/ppermute | solution.py:336
  123.1 0.7 copy-done.11
  123.7 0.8 copy.63.wcol_ref
  124.6 0.7 reshape.775
  125.3 0.8 copy.62
  126.1 3.1 %collective-permute-done.4 = bf16[144,512]{1,0:T(8,128)(2,1)} collective-permute-done((bf16[144,512]{1,0:T(8,128)(2,1)}, bf16[144,512]{1,0:T(8,128)(2,1)}, u32[]{:S(2)}, u32[]{:S(2)}) %collective-permute-start.4) | collective-permute-done | bytes 147488 | tf_op jit(solution)/shard_map/ppermute | solution.py:336
  129.2 8.3 %collective-permute-done.2 = bf16[144,512]{1,0:T(8,128)(2,1)} collective-permute-done((bf16[144,512]{1,0:T(8,128)(2,1)}, bf16[144,512]{1,0:T(8,128)(2,1)}, u32[]{:S(2)}, u32[]{:S(2)}) %collective-permute-start.2) | collective-permute-done | bytes 147488 | tf_op jit(solution)/shard_map/ppermute | solution.py:336
  137.5 0.5 collective-permute-done.1
  138.0 4.7 %collective-permute-done = bf16[144,512]{1,0:T(8,128)(2,1)} collective-permute-done((bf16[144,512]{1,0:T(8,128)(2,1)S(1)}, bf16[144,512]{1,0:T(8,128)(2,1)}, u32[]{:S(2)}, u32[]{:S(2)}) %collective-permute-start) | collective-permute-done | bytes 147488 | tf_op jit(solution)/shard_map/ppermute | solution.py:336
  142.7 1.4 convert_add_fusion
  144.1 0.5 slice.32
  144.6 1.9 %subtract_convert_fusion.1 = (bf16[128,512]{1,0:T(8,128)(2,1)S(1)}, f32[128,512]{1,0:T(8,128)}, f32[128,512]{1,0:T(8,128)}) fusion(f32[144,512]{1,0:T(8,128)S(1)} %convert_add_fusion, f32[128,512]{1,0:T(8,128)S(1)} %copy-done.6, f32[128,512]{1,0:T(8,128)S(1)} %copy-done.8, bf16[512,512]{1,0:T(8,128)(2,1)} %param.12, s32[]{:T(128)S(6)} %select_n.254), kind=kLoop, calls=%fused_computation.90 | loop fusion | flops 983040 | bytes 1572868 | tf_op jit(solution)/shard_map/convert_element_type | solution.py:33
  146.5 0.3 collective-permute-start.7
  146.8 2.6 %collective-permute-start.8 = (bf16[128,512]{1,0:T(8,128)(2,1)S(1)}, bf16[128,512]{1,0:T(8,128)(2,1)}, u32[]{:S(2)}, u32[]{:S(2)}) collective-permute-start(bf16[128,512]{1,0:T(8,128)(2,1)S(1)} %get-tuple-element.266), channel_id=1, source_target_pairs={{0,2},{1,3},{2,0},{3,1},{4,6},{5,7},{6,4},{7,5},{8,10},{9,11},{10,... | collective-permute-start | bytes 393224 | tf_op jit(solution)/shard_map/ppermute | solution.py:349
  149.4 1.8 %collective-permute-start.9 = (bf16[128,512]{1,0:T(8,128)(2,1)S(1)}, bf16[128,512]{1,0:T(8,128)(2,1)}, u32[]{:S(2)}, u32[]{:S(2)}) collective-permute-start(bf16[128,512]{1,0:T(8,128)(2,1)S(1)} %get-tuple-element.266), channel_id=1, source_target_pairs={{0,1},{1,2},{2,3},{3,0},{4,5},{5,6},{6,7},{7,4},{8,9},{9,10},{10,1... | collective-permute-start | bytes 393224 | tf_op jit(solution)/shard_map/ppermute | solution.py:349
  151.9 11.9 %shard_map.108 = bf16[320,2048]{1,0:T(8,128)(2,1)} custom-call(s32[320,4]{1,0:T(8,128)S(1)} %bitcast.90, s32[320,4]{1,0:T(8,128)S(1)} %add_select_fusion.3.pcol_ref, f32[320,4]{1,0:T(8,128)S(1)} %copy.63.wcol_ref, bf16[2560,512]{1,0:T(8,128)(2,1)S(1)} %bitcast.87, bf16[4,512,2048]{2,1,0:T(8,128)(2,1)} %proj_ref.3), custom_call_target="tpu_custom_call" | custom-call | flops 6039797760 | bytes 13000000 | tf_op jit(solution)/shard_map/pallas_call | solution.py:355
  163.9 1.9 %conditional.1 = (bf16[320,2048]{1,0:T(8,128)(2,1)}, f32[128,512]{1,0:T(8,128)}, f32[128,512]{1,0:T(8,128)}, bf16[512,512]{1,0:T(8,128)(2,1)S(1)}) conditional(s32[]{:T(128)} %bitcast.32, (s32[]{:T(128)}, s32[4,1,1]{0,2,1:T(1,128)S(1)}, bf16[128,512]{1,0:T(8,128)(2,1)S(1)}, s32[]{:T(128)}, s32[4,1,1]{0,2,1:T(1,128)S(1)}, ...), branch_computations={%region_0.1_spmd, %region_1.10_spmd} | conditional | flops 5392036352 | bytes 83117216 | solution.py:378
  164.1 0.1 broadcast_bitcast_fusion.2
  164.2 1.3 fusion.2
  165.8 0.8 copy.81
  (37 shorter events, 0.6 us)
Async XLA Ops:
  9.2 22.7 %all-to-all-start.4 = ((s32[32,1,128]{2,1,0:T(1,128)}), s32[32,1,128]{2,1,0:T(1,128)S(1)}, u32[]{:S(2)}, u32[]{:S(2)}) async-start(s32[32,1,128]{2,1,0:T(1,128)} %bitcast.26), calls=%async_computation.5 | async-start | bytes 32768 | tf_op jit(solution)/shard_map/all_to_all | solution.py:282
  30.4 1.5 copy-start.2
  32.0 60.6 %all-to-all-start.5 = ((bf16[32,80,512]{2,1,0:T(8,128)(2,1)}), bf16[32,80,512]{2,1,0:T(8,128)(2,1)S(1)}, u32[]{:S(2)}, u32[]{:S(2)}) async-start(bf16[32,80,512]{2,1,0:T(8,128)(2,1)} %bitcast.89), calls=%async_computation.6 | async-start | bytes 5242880 | tf_op jit(solution)/shard_map/all_to_all | solution.py:303
  39.4 44.6 %all-gather.2.cloned.1.call-start = ((), (), s32[]{:S(2)}) async-start(), calls=%async_computation.9 | async-start | bytes 1179648 | tf_op jit(solution)/shard_map/all_gather | solution.py:264
  84.0 1.3 copy-start.3
  85.3 1.2 copy-start.4
  92.6 1.5 copy-start
  94.1 57.7 %all-to-all-start.6 = ((bf16[32,80,512]{2,1,0:T(8,128)(2,1)}), bf16[32,80,512]{2,1,0:T(8,128)(2,1)S(1)}, u32[]{:S(2)}, u32[]{:S(2)}) async-start(bf16[32,80,512]{2,1,0:T(8,128)(2,1)} %bitcast.34), calls=%async_computation.7 | async-start | bytes 5242880 | tf_op jit(solution)/shard_map/all_to_all | solution.py:323
  101.7 1.7 %copy-start.1 = (bf16[32,80,512]{2,1,0:T(8,128)(2,1)S(1)}, bf16[32,80,512]{2,1,0:T(8,128)(2,1)}, u32[]{:S(2)}) copy-start(bf16[32,80,512]{2,1,0:T(8,128)(2,1)} %copy-done) | copy-start | bytes 7864324
  107.0 10.0 %collective-permute-start.6 = (bf16[144,512]{1,0:T(8,128)(2,1)S(1)}, bf16[144,512]{1,0:T(8,128)(2,1)S(1)}, u32[]{:S(2)}, u32[]{:S(2)}) collective-permute-start(bf16[144,512]{1,0:T(8,128)(2,1)S(1)} %get-tuple-element.226), channel_id=1, source_target_pairs={{0,56},{8,0},{16,8},{24,16},{32,24},{40,32},{48,40},{56,48},{1,57}... | collective-permute-start | bytes 442376 | tf_op jit(solution)/shard_map/ppermute | solution.py:336
  108.6 14.5 %collective-permute-start.5 = (bf16[144,512]{1,0:T(8,128)(2,1)S(1)}, bf16[144,512]{1,0:T(8,128)(2,1)S(1)}, u32[]{:S(2)}, u32[]{:S(2)}) collective-permute-start(bf16[144,512]{1,0:T(8,128)(2,1)S(1)} %get-tuple-element.225), channel_id=1, source_target_pairs={{0,48},{8,56},{16,0},{24,8},{32,16},{40,24},{48,32},{56,40},{1,49}... | collective-permute-start | bytes 442376 | tf_op jit(solution)/shard_map/ppermute | solution.py:336
  110.5 18.6 %collective-permute-start.4 = (bf16[144,512]{1,0:T(8,128)(2,1)}, bf16[144,512]{1,0:T(8,128)(2,1)}, u32[]{:S(2)}, u32[]{:S(2)}) collective-permute-start(bf16[144,512]{1,0:T(8,128)(2,1)} %get-tuple-element.224), channel_id=1, source_target_pairs={{0,40},{8,48},{16,56},{24,0},{32,8},{40,16},{48,24},{56,32},{1,41}... | collective-permute-start | bytes 442376 | tf_op jit(solution)/shard_map/ppermute | solution.py:336
  112.7 16.5 %collective-permute-start.3 = (bf16[144,512]{1,0:T(8,128)(2,1)}, bf16[144,512]{1,0:T(8,128)(2,1)}, u32[]{:S(2)}, u32[]{:S(2)}) collective-permute-start(bf16[144,512]{1,0:T(8,128)(2,1)} %get-tuple-element.223), channel_id=1, source_target_pairs={{0,32},{8,40},{16,48},{24,56},{32,0},{40,8},{48,16},{56,24},{1,33}... | collective-permute-start | bytes 442376 | tf_op jit(solution)/shard_map/ppermute | solution.py:336
  115.2 22.3 %collective-permute-start.2 = (bf16[144,512]{1,0:T(8,128)(2,1)}, bf16[144,512]{1,0:T(8,128)(2,1)}, u32[]{:S(2)}, u32[]{:S(2)}) collective-permute-start(bf16[144,512]{1,0:T(8,128)(2,1)} %get-tuple-element.222), channel_id=1, source_target_pairs={{0,24},{8,32},{16,40},{24,48},{32,56},{40,0},{48,8},{56,16},{1,25}... | collective-permute-start | bytes 442376 | tf_op jit(solution)/shard_map/ppermute | solution.py:336
  117.0 6.1 %copy-start.10 = (bf16[144,512]{1,0:T(8,128)(2,1)}, bf16[144,512]{1,0:T(8,128)(2,1)S(1)}, u32[]{:S(2)}) copy-start(bf16[144,512]{1,0:T(8,128)(2,1)S(1)} %collective-permute-done.6) | copy-start | bytes 442372
  117.0 20.9 %collective-permute-start.1 = (bf16[144,512]{1,0:T(8,128)(2,1)S(1)}, bf16[144,512]{1,0:T(8,128)(2,1)}, u32[]{:S(2)}, u32[]{:S(2)}) collective-permute-start(bf16[144,512]{1,0:T(8,128)(2,1)S(1)} %get-tuple-element.221), channel_id=1, source_target_pairs={{0,16},{8,24},{16,32},{24,40},{32,48},{40,56},{48,0},{56,8},{1,17}... | collective-permute-start | bytes 442376 | tf_op jit(solution)/shard_map/ppermute | solution.py:336
  123.1 0.7 copy-start.11
  123.7 18.9 %collective-permute-start = (bf16[144,512]{1,0:T(8,128)(2,1)S(1)}, bf16[144,512]{1,0:T(8,128)(2,1)}, u32[]{:S(2)}, u32[]{:S(2)}) collective-permute-start(bf16[144,512]{1,0:T(8,128)(2,1)S(1)} %get-tuple-element.220), channel_id=1, source_target_pairs={{0,8},{8,16},{16,24},{24,32},{32,40},{40,48},{48,56},{56,0},{1,9},... | collective-permute-start | bytes 442376 | tf_op jit(solution)/shard_map/ppermute | solution.py:336
  126.1 18.6 %copy-start.6 = (f32[128,512]{1,0:T(8,128)S(1)}, f32[128,512]{1,0:T(8,128)}, u32[]{:S(2)}) copy-start(f32[128,512]{1,0:T(8,128)} %param.13) | copy-start | bytes 786436
  126.1 18.6 %copy-start.8 = (f32[128,512]{1,0:T(8,128)S(1)}, f32[128,512]{1,0:T(8,128)}, u32[]{:S(2)}) copy-start(f32[128,512]{1,0:T(8,128)} %param.14) | copy-start | bytes 786436
  146.5 17.3 %collective-permute-start.7 = (bf16[128,512]{1,0:T(8,128)(2,1)S(1)}, bf16[128,512]{1,0:T(8,128)(2,1)S(1)}, u32[]{:S(2)}, u32[]{:S(2)}) collective-permute-start(bf16[128,512]{1,0:T(8,128)(2,1)S(1)} %get-tuple-element.266), channel_id=1, source_target_pairs={{0,3},{1,0},{2,1},{3,2},{4,7},{5,4},{6,5},{7,6},{8,11},{9,8},{10,9... | collective-permute-start | bytes 393224 | tf_op jit(solution)/shard_map/ppermute | solution.py:349
  146.8 17.0 %collective-permute-start.8 = (bf16[128,512]{1,0:T(8,128)(2,1)S(1)}, bf16[128,512]{1,0:T(8,128)(2,1)}, u32[]{:S(2)}, u32[]{:S(2)}) collective-permute-start(bf16[128,512]{1,0:T(8,128)(2,1)S(1)} %get-tuple-element.266), channel_id=1, source_target_pairs={{0,2},{1,3},{2,0},{3,1},{4,6},{5,7},{6,4},{7,5},{8,10},{9,11},{10,... | collective-permute-start | bytes 393224 | tf_op jit(solution)/shard_map/ppermute | solution.py:349
  149.4 14.4 %collective-permute-start.9 = (bf16[128,512]{1,0:T(8,128)(2,1)S(1)}, bf16[128,512]{1,0:T(8,128)(2,1)}, u32[]{:S(2)}, u32[]{:S(2)}) collective-permute-start(bf16[128,512]{1,0:T(8,128)(2,1)S(1)} %get-tuple-element.266), channel_id=1, source_target_pairs={{0,1},{1,2},{2,3},{3,0},{4,5},{5,6},{6,7},{7,4},{8,9},{9,10},{10,1... | collective-permute-start | bytes 393224 | tf_op jit(solution)/shard_map/ppermute | solution.py:349
  151.9 12.0 %copy-start.12 = (s32[320,4]{0,1:T(4,128)S(1)}, s32[320,4]{0,1:T(4,128)}, u32[]{:S(2)}) copy-start(s32[320,4]{0,1:T(4,128)} %param.9) | copy-start | bytes 15364
  151.9 12.0 %copy-start.13 = (bf16[320,4]{0,1:T(4,128)(2,1)S(1)}, bf16[320,4]{0,1:T(4,128)(2,1)}, u32[]{:S(2)}) copy-start(bf16[320,4]{0,1:T(4,128)(2,1)} %param.10) | copy-start | bytes 7684
Sparse Core Ops, SparseCore 0:
  42.7 41.2 all-gather.1

commit v3 on v2

--- a/solution.py
+++ b/solution.py
@@ -19,8 +19,7 @@
 CORES = 2
 CAP = 80
 LANES = 128
-FLAG_ROWS = 16
-VMEM = 40 * 1024 * 1024
+OVER = 1e30
 BF = jnp.bfloat16
 F32 = jnp.float32
 NT = (((1,), (1,)), ((), ()))
@@ -96,14 +95,19 @@
     )
     quarter = first_moment.shape[0]
     start = lax.axis_index("x") * quarter
-    share = lax.psum_scatter(slab_grad, "x", scatter_dimension=0, tiled=True)
+    share = jnp.sum(
+        lax.all_to_all(
+            slab_grad.reshape(-1, quarter, width), "x", split_axis=0, concat_axis=0, tiled=True
+        ),
+        axis=0,
+    )
     old_rows = lax.dynamic_slice_in_dim(values, start, quarter, 0)
     new_first, new_second, new_part = adam_rows(old_rows, share, first_moment, second_moment)
     new_values = lax.all_gather(new_part, "x", axis=0, tiled=True)
     return (layer_out, new_values, new_first, new_second)
 
 
-def call(kernel, out_shape, grid=None, in_specs=None, out_specs=None, scratch=(), cost=None):
+def call(kernel, out_shape, vmem, grid=None, in_specs=None, out_specs=None, scratch=(), cost=None):
     extra = {} if grid is None else {"grid": grid}
     if in_specs is not None:
         extra["in_specs"] = in_specs
@@ -113,7 +117,7 @@
         kernel,
         out_shape=out_shape,
         scratch_shapes=list(scratch),
-        compiler_params=pltpu.CompilerParams(vmem_limit_bytes=VMEM),
+        compiler_params=pltpu.CompilerParams(vmem_limit_bytes=vmem * 1024 * 1024),
         cost_estimate=cost,
         **extra,
     )
@@ -156,64 +160,60 @@
 
 
 def send_kernel(
-    cells, tok, tg_ref, proj_ref, pcol_ref, cell_ref, rank_ref, wt_ref, out_ref, chosen, place
+    group, projs, tg_ref, proj_ref, pcol_ref, cell_ref, rank_ref, wt_ref, out_ref, chosen, place
 ):
     step = pl.program_id(0)
-    per_token = pcol_ref.shape[1]
-    back = lax.dot_general(tg_ref[...], proj_ref[0], NT, preferred_element_type=F32)
-    back = back.astype(BF)
-    for j in range(per_token):
-        mine = pcol_ref[:, j : j + 1] == step
-        span = pl.ds(j * tok, tok)
-
-        @pl.when(step == 0)
-        def _():
-            chosen[span, :] = back
-
-        @pl.when(step > 0)
-        def _():
-            chosen[span, :] = jnp.where(mine, back, chosen[span, :])
-
-    @pl.when(step == pl.num_programs(0) - 1)
+    tok, per_token = pcol_ref.shape
+
+    @pl.when(step == 0)
     def _():
         count = cell_ref.shape[1]
         at = lax.broadcasted_iota(jnp.int32, (CAP, count), 0) == rank_ref[...]
         place[...] = jnp.where(at, wt_ref[...].astype(F32), 0.0).astype(BF)
-        group = 4
-        for g in range(cells // group):
-            parts = []
-            for d in range(g * group, (g + 1) * group):
-                here = (cell_ref[...] == d).astype(F32).astype(BF)
-                parts.append(place[...] * here)
-            pick = jnp.concatenate(parts, axis=0)
-            out_ref[pl.ds(g * group * CAP, group * CAP), :] = jnp.dot(
-                pick, chosen[...], preferred_element_type=F32
-            ).astype(BF)
-
-
-def look_kernel(ids_ref, table_ref, out_ref):
-    rows = ids_ref.shape[0]
-    total = table_ref.shape[0]
-    pick = lax.broadcasted_iota(jnp.int32, (rows, total), 1) == ids_ref[...]
+
+    @pl.when(step < projs)
+    def _():
+        back = lax.dot_general(tg_ref[...], proj_ref[0], NT, preferred_element_type=F32)
+        back = back.astype(BF)
+        for j in range(per_token):
+            mine = (pcol_ref[:, j : j + 1] == step) | (step == 0)
+            span = pl.ds(j * tok, tok)
+            chosen[span, :] = jnp.where(mine, back, chosen[span, :])
+
+    @pl.when(step >= projs)
+    def _():
+        first = (step - projs) * group
+        parts = []
+        for d in range(group):
+            here = (cell_ref[...] == first + d).astype(F32).astype(BF)
+            parts.append(place[...] * here)
+        pick = jnp.concatenate(parts, axis=0)
+        out_ref[...] = jnp.dot(pick, chosen[...], preferred_element_type=F32).astype(BF)
+
+
+def look_kernel(ids_ref, *refs):
+    *pieces, out_ref, table = refs
+    rows = pieces[0].shape[0]
+
+    @pl.when(pl.program_id(0) == 0)
+    def _():
+        for k, piece in enumerate(pieces):
+            table[pl.ds(k * rows, rows), :] = piece[...]
+
+    pick = lax.broadcasted_iota(jnp.int32, (ids_ref.shape[0], table.shape[0]), 1) == ids_ref[...]
     out_ref[...] = jnp.dot(
-        pick.astype(F32).astype(BF), table_ref[...], preferred_element_type=F32
+        pick.astype(F32).astype(BF), table[...], preferred_element_type=F32
     ).astype(BF)
 
 
-def sum_kernel(ids_ref, flags_ref, z_ref, got_ref, *out_refs):
-    depth = len(out_refs)
-    rows = out_refs[0].shape[0] - FLAG_ROWS
+def sum_kernel(ids_ref, flags_ref, got_ref, *out_refs):
+    rows = out_refs[0].shape[0]
     slots = ids_ref.shape[1]
-    over = jnp.max(flags_ref[...]).astype(F32)
+    over = jnp.where(jnp.max(flags_ref[...]) > 0, OVER, 0.0)
     for k, out_ref in enumerate(out_refs):
-        base = lax.rem(z_ref[0] + k, depth) * rows
-        pick = lax.broadcasted_iota(jnp.int32, (rows, slots), 0) == ids_ref[...] - base
-        out_ref[:rows, :] = jnp.dot(
-            pick.astype(F32).astype(BF), got_ref[...], preferred_element_type=F32
-        ).astype(out_ref.dtype)
-        out_ref[rows:, :] = jnp.full((FLAG_ROWS, out_ref.shape[1]), over, F32).astype(
-            out_ref.dtype
-        )
+        pick = lax.broadcasted_iota(jnp.int32, (rows, slots), 0) == ids_ref[...] - k * rows
+        part = jnp.dot(pick.astype(F32).astype(BF), got_ref[...], preferred_element_type=F32)
+        out_ref[...] = (part + over).astype(out_ref.dtype)
 
 
 def out_kernel(slot_ref, pcol_ref, wcol_ref, ret_ref, proj_ref, out_ref, picked, total):
@@ -261,15 +261,14 @@
     table_rows = depth * quarter
     start = lax.axis_index("x") * quarter
     old_rows = lax.dynamic_slice_in_dim(values, start, quarter, 0)
-    table = lax.all_gather(old_rows, "z", axis=0, tiled=True)
 
     by_pick = picks.T.reshape(1, total)
-    owner = by_pick // rows_dev
-    row = by_pick % rows_dev
-    owner_y = owner // (depth * CORES)
-    owner_z = (owner // CORES) % depth
-    cell = (owner_y * CORES + owner % CORES) * parts + row // quarter
-    trow = owner_z * quarter + row % quarter
+    owner = lax.div(by_pick, rows_dev)
+    row = lax.rem(by_pick, rows_dev)
+    owner_y = lax.div(owner, depth * CORES)
+    owner_z = lax.rem(lax.div(owner, CORES), depth)
+    cell = (owner_y * CORES + lax.rem(owner, CORES)) * parts + lax.div(row, quarter)
+    trow = owner_z * quarter + lax.rem(row, quarter)
     block = 256
     rank, requests = call(
         functools.partial(rank_kernel, cells, block),
@@ -277,26 +276,33 @@
             jax.ShapeDtypeStruct((1, total), jnp.int32),
             jax.ShapeDtypeStruct((cells, LANES), jnp.int32),
         ),
+        8,
         cost=cost(2 * total * cells * 400, 20000),
     )(cell, trow)
     received = lax.all_to_all(requests, plane, split_axis=0, concat_axis=0, tiled=True)
 
-    pcol = picks % proj_count
+    pcol = lax.rem(picks, proj_count)
     wt_row = pick_weights.T.reshape(1, total)
     whole = lambda shape: pl.BlockSpec(shape, lambda i: (0,) * len(shape))
+    group = 4
     sent = call(
-        functools.partial(send_kernel, cells, tok),
+        functools.partial(send_kernel, group, proj_count),
         jax.ShapeDtypeStruct((slots, width), BF),
-        grid=(proj_count,),
+        24,
+        grid=(proj_count + cells // group,),
         in_specs=[
             whole((tok, out_width)),
-            pl.BlockSpec((1, width, out_width), lambda i: (i, 0, 0)),
+            pl.BlockSpec(
+                (1, width, out_width), lambda i: (jnp.minimum(i, proj_count - 1), 0, 0)
+            ),
             whole((tok, per_token)),
             whole((1, total)),
             whole((1, total)),
             whole((1, total)),
         ],
-        out_specs=whole((slots, width)),
+        out_specs=pl.BlockSpec(
+            (group * CAP, width), lambda i: (jnp.maximum(i - proj_count, 0), 0)
+        ),
         scratch=[pltpu.VMEM((total, width), BF), pltpu.VMEM((CAP, total), BF)],
         cost=cost(2 * width * (tok * proj_count * out_width + slots * total), 12000000),
     )(token_grads, projectors, pcol, cell, rank, wt_row)
@@ -304,43 +310,47 @@
         sent.reshape(cells, CAP, width), plane, split_axis=0, concat_axis=0, tiled=True
     ).reshape(slots, width)
 
-    asked = received[:, :CAP]
+    pieces = [old_rows] + [
+        lax.ppermute(old_rows, "z", [(i, (i - k) % depth) for i in range(depth)])
+        for k in range(1, depth)
+    ]
+    z_here = lax.axis_index("z")
+    told = received[:, :CAP]
+    from_z = lax.rem(lax.div(told, quarter) + depth - z_here, depth)
+    asked = jnp.where(told < 0, -1, from_z * quarter + lax.rem(told, quarter))
     flags = received[:, LANES - 1 :]
     vmem = pl.BlockSpec(memory_space=pltpu.VMEM)
     chunk = slots // 8
     looked = call(
         look_kernel,
         jax.ShapeDtypeStruct((slots, width), BF),
+        16,
         grid=(8,),
-        in_specs=[
-            pl.BlockSpec((chunk, 1), lambda i: (i, 0)),
-            whole((table_rows, width)),
-        ],
+        in_specs=[pl.BlockSpec((chunk, 1), lambda i: (i, 0))] + [whole((quarter, width))] * depth,
         out_specs=pl.BlockSpec((chunk, width), lambda i: (i, 0)),
+        scratch=[pltpu.VMEM((table_rows, width), BF)],
         cost=cost(2 * width * slots * table_rows, 4000000),
-    )(asked.reshape(slots, 1), table)
+    )(asked.reshape(slots, 1), *pieces)
     got, looked = lax.optimization_barrier((got, looked))
     returned = lax.all_to_all(
         looked.reshape(cells, CAP, width), plane, split_axis=0, concat_axis=0, tiled=True
     ).reshape(slots, width)
 
-    z_here = lax.axis_index("z").reshape(1)
     sums = call(
         sum_kernel,
-        (jax.ShapeDtypeStruct((quarter + FLAG_ROWS, width), BF),) * depth,
-        in_specs=[vmem, vmem, pl.BlockSpec(memory_space=pltpu.SMEM), vmem],
+        (jax.ShapeDtypeStruct((quarter, width), BF),) * depth,
+        16,
+        in_specs=[vmem] * 3,
         out_specs=(vmem,) * depth,
         cost=cost(2 * width * slots * table_rows, 4000000),
-    )(asked.reshape(1, slots), flags, z_here, got)
+    )(asked.reshape(1, slots), flags, got)
     shares = [sums[0]] + [
         lax.ppermute(sums[k], "z", [(i, (i + k) % depth) for i in range(depth)])
         for k in range(1, depth)
     ]
     share = functools.reduce(lambda p, q: p + q, [s.astype(F32) for s in shares])
-    flag = share[quarter, 0]
-    new_first, new_second, new_part = adam_rows(
-        old_rows, share[:quarter], first_moment, second_moment
-    )
+    flag = share[0, 0] > 0.5 * OVER
+    new_first, new_second, new_part = adam_rows(old_rows, share, first_moment, second_moment)
     x_here = lax.axis_index("x")
     new_values = jnp.zeros((parts, quarter, width), BF)
     for k in range(parts):
@@ -355,6 +365,7 @@
     layer_out = call(
         out_kernel,
         jax.ShapeDtypeStruct((tok, out_width), BF),
+        32,
         grid=(proj_count,),
         in_specs=[
             whole((tok, per_token)),
@@ -375,7 +386,7 @@
 
 def on_device(*args):
     flag, outs = short_way(*args)
-    return lax.cond(flag > 0.5, lambda given, done: long_way(*given), lambda given, done: done, args, outs)
+    return lax.cond(flag, lambda given, done: long_way(*given), lambda given, done: done, args, outs)
 
 
 def solution(mesh):

time: 174 us -> 148 us (0.85)
  waiting for transfers between devices: 60.4 us -> 34.8 us
  starting transfers between devices: 40.8 us -> 58 us
  between operations: 14.9 us -> 1.45 us
  local copies, waits for them, and re-layouts: 17.9 us -> 13.9 us
    all_gather x1 -> x0, waiting for transfers between devices: 41.3 us -> none  [short_way(): table = lax.all_gather(old_rows, 'z', axis=0, tiled=True)]
    ppermute x0 -> x7, waiting for transfers between devices: none -> 18.1 us  [short_way(): lax.ppermute(old_rows, 'z', [(i, (i - k) % depth) for i in range(depth)])]
    ppermute x0 -> x7, starting transfers between devices: none -> 16.6 us  [short_way(): lax.ppermute(old_rows, 'z', [(i, (i - k) % depth) for i in range(depth)])]
    ppermute x7, waiting for transfers between devices: 19 us -> 16.7 us  [short_way(): lax.ppermute(sums[k], 'z', [(i, (i + k) % depth) for i in range(depth)])]
    unnamed x24 -> x18, local copies, waits for them, and re-layouts: 9.66 us -> 8.46 us
  transfers between devices with their start and end apart: 14 -> 20, of which waited for: 6 -> 9; matrix products, arithmetic and copies ran while one was open for 7% -> 5% of each run, Pallas kernels for 19% -> 23%
where the time goes in v3:
time: 148 us
  starting transfers between devices  58 us (39%)
  Pallas kernels  35.2 us (24%)
  waiting for transfers between devices  34.8 us (24%)
  local copies, waits for them, and re-layouts  13.9 us (9%)
  other arithmetic  3.9 us (3%)
    ppermute x7, waiting for transfers between devices, short_way(): lax.ppermute(old_rows, 'z', [(i, (i - k) % depth) for i in range(depth)])  18.1 us
    ppermute x7, waiting for transfers between devices, short_way(): lax.ppermute(sums[k], 'z', [(i, (i + k) % depth) for i in range(depth)])  16.7 us
    ppermute x7, starting transfers between devices, short_way(): lax.ppermute(old_rows, 'z', [(i, (i - k) % depth) for i in range(depth)])  16.6 us
    ppermute x7, starting transfers between devices, short_way(): lax.ppermute(sums[k], 'z', [(i, (i + k) % depth) for i in range(depth)])  14.3 us
    pallas_call x1, Pallas kernels, short_way(): call(out_kernel, jax.ShapeDtypeStruct((tok, out_width), BF), 32, grid=(pr...  11.9 us
    pallas_call x1, Pallas kernels, short_way(): call(functools.partial(send_kernel, group, proj_count), jax.ShapeDtypeStr...  11.5 us
    unnamed x18, local copies, waits for them, and re-layouts  8.46 us
    all_to_all x1, starting transfers between devices, short_way(): lax.all_to_all(requests, plane, split_axis=0, concat_axis=0, tiled=True)  7.62 us
  transfers between devices with their start and end apart: 20, of which 9 were waited for; matrix products, arithmetic and copies ran while one was open for 5% of the time, Pallas kernels for 23%

profile of v3, /device:TPU:2, one launch (start us, length us, event | category | flops | bytes accessed | tf_op | source)
XLA Modules:
  0.0 147.5 jit_solution(15338187201450593462)
XLA Ops:
  0.6 0.8 reshape.544
  1.5 1.1 shard_map.104
  2.6 7.6 %all-to-all-start.5 = ((s32[32,1,128]{2,1,0:T(1,128)}), s32[32,1,128]{2,1,0:T(1,128)S(1)}, u32[]{:S(2)}, u32[]{:S(2)}) async-start(s32[32,1,128]{2,1,0:T(1,128)} %bitcast.27), calls=%async_computation.5 | async-start | bytes 32768 | tf_op jit(solution)/shard_map/all_to_all | solution.py:282
  10.3 0.8 copy.64
  11.1 0.8 reshape.547.wt_ref
  11.9 11.5 %shard_map.105 = bf16[2560,512]{1,0:T(8,128)(2,1)S(1)} custom-call(bf16[320,2048]{1,0:T(8,128)(2,1)} %tg_ref.1, bf16[4,512,2048]{2,1,0:T(8,128)(2,1)} %proj_ref.3, s32[320,4]{1,0:T(8,128)S(1)} %negate_select_fusion.8.pcol_ref, s32[1,1280]{1,0:T(1,128)S(1)} %fusion.46.cell_ref, s32[1,1280]{1,0:T(1,128)S(1)} %get-tuple-element.217.rank_ref, ...), custom_call_target="tpu_custom_call" | custom-call | flops 6039797760 | bytes 12000000 | tf_op jit(solution)/shard_map/pallas_call | solution.py:288
  23.5 1.6 %copy-done.2 = bf16[2560,512]{1,0:T(8,128)(2,1)} copy-done((bf16[2560,512]{1,0:T(8,128)(2,1)}, bf16[2560,512]{1,0:T(8,128)(2,1)S(1)}, u32[]{:S(2)}) %copy-start.2) | copy-done | bytes 2621464
  25.0 7.4 %all-to-all-start.6 = ((bf16[32,80,512]{2,1,0:T(8,128)(2,1)}), bf16[32,80,512]{2,1,0:T(8,128)(2,1)S(1)}, u32[]{:S(2)}, u32[]{:S(2)}) async-start(bf16[32,80,512]{2,1,0:T(8,128)(2,1)} %bitcast.88), calls=%async_computation.6 | async-start | bytes 5242880 | tf_op jit(solution)/shard_map/all_to_all | solution.py:309
  32.4 0.9 constant_dynamic-slice_fusion.refs_0_
  33.3 5.9 %collective-permute-start = (bf16[128,512]{1,0:T(8,128)(2,1)S(1)}, bf16[128,512]{1,0:T(8,128)(2,1)S(1)}, u32[]{:S(2)}, u32[]{:S(2)}) collective-permute-start(bf16[128,512]{1,0:T(8,128)(2,1)S(1)} %constant_dynamic-slice_fusion.refs_0_), channel_id=1, source_target_pairs={{0,56},{8,0},{16,8},{24,16},{32,24},{40,32},{48,40},{56,48},{1,57}... | collective-permute-start | bytes 393224 | tf_op jit(solution)/shard_map/ppermute | solution.py:314
  39.3 1.5 collective-permute-start.1
  40.7 0.4 collective-permute-start.2
  41.2 5.0 %collective-permute-start.3 = (bf16[128,512]{1,0:T(8,128)(2,1)S(1)}, bf16[128,512]{1,0:T(8,128)(2,1)S(1)}, u32[]{:S(2)}, u32[]{:S(2)}) collective-permute-start(bf16[128,512]{1,0:T(8,128)(2,1)S(1)} %constant_dynamic-slice_fusion.refs_0_), channel_id=1, source_target_pairs={{0,32},{8,40},{16,48},{24,56},{32,0},{40,8},{48,16},{56,24},{1,33}... | collective-permute-start | bytes 393224 | tf_op jit(solution)/shard_map/ppermute | solution.py:314
  46.2 2.5 %collective-permute-start.5 = (bf16[128,512]{1,0:T(8,128)(2,1)S(1)}, bf16[128,512]{1,0:T(8,128)(2,1)}, u32[]{:S(2)}, u32[]{:S(2)}) collective-permute-start(bf16[128,512]{1,0:T(8,128)(2,1)S(1)} %constant_dynamic-slice_fusion.refs_0_), channel_id=1, source_target_pairs={{0,16},{8,24},{16,32},{24,40},{32,48},{40,56},{48,0},{56,8},{1,17}... | collective-permute-start | bytes 393224 | tf_op jit(solution)/shard_map/ppermute | solution.py:314
  48.7 1.3 collective-permute-done.1.refs_2_
  50.0 1.3 collective-permute-start.6
  51.3 1.7 %reshape.618.ids_ref = s32[2560,1]{1,0:T(8,128)} reshape(s32[32,80]{1,0:T(8,128)S(1)} %fusion.43) | data formatting | bytes 20480 | tf_op jit(solution)/shard_map/reshape | solution.py:333
  52.9 9.1 %collective-permute-done.2.refs_3_ = bf16[128,512]{1,0:T(8,128)(2,1)S(1)} collective-permute-done((bf16[128,512]{1,0:T(8,128)(2,1)S(1)}, bf16[128,512]{1,0:T(8,128)(2,1)S(1)}, u32[]{:S(2)}, u32[]{:S(2)}) %collective-permute-start.2) | collective-permute-done | bytes 131104 | tf_op jit(solution)/shard_map/ppermute | solution.py:314
  62.0 2.9 %collective-permute-done.4.refs_5_ = bf16[128,512]{1,0:T(8,128)(2,1)} collective-permute-done((bf16[128,512]{1,0:T(8,128)(2,1)S(1)}, bf16[128,512]{1,0:T(8,128)(2,1)}, u32[]{:S(2)}, u32[]{:S(2)}) %collective-permute-start.4) | collective-permute-done | bytes 131104 | tf_op jit(solution)/shard_map/ppermute | solution.py:314
  64.9 2.8 %collective-permute-done.5.refs_6_ = bf16[128,512]{1,0:T(8,128)(2,1)} collective-permute-done((bf16[128,512]{1,0:T(8,128)(2,1)S(1)}, bf16[128,512]{1,0:T(8,128)(2,1)}, u32[]{:S(2)}, u32[]{:S(2)}) %collective-permute-start.5) | collective-permute-done | bytes 131104 | tf_op jit(solution)/shard_map/ppermute | solution.py:314
  67.8 1.9 %collective-permute-done.6.refs_7_ = bf16[128,512]{1,0:T(8,128)(2,1)} collective-permute-done((bf16[128,512]{1,0:T(8,128)(2,1)S(1)}, bf16[128,512]{1,0:T(8,128)(2,1)}, u32[]{:S(2)}, u32[]{:S(2)}) %collective-permute-start.6) | collective-permute-done | bytes 131104 | tf_op jit(solution)/shard_map/ppermute | solution.py:314
  69.7 1.3 copy-done.3
  71.0 7.2 %shard_map.106 = bf16[2560,512]{1,0:T(8,128)(2,1)} custom-call(s32[2560,1]{1,0:T(8,128)S(1)} %copy-done.3, bf16[128,512]{1,0:T(8,128)(2,1)S(1)} %constant_dynamic-slice_fusion.refs_0_, bf16[128,512]{1,0:T(8,128)(2,1)S(1)} %collective-permute-done.refs_1_, bf16[128,512]{1,0:T(8,128)(2,1)S(1)} %collective-permute-done.1.refs_2_, ...), custom_call_target="tpu_custom_call" | custom-call | flops 2684354560 | bytes 4000000 | tf_op jit(solution)/shard_map/pallas_call | solution.py:324
  78.1 1.6 %copy-done = bf16[32,80,512]{2,1,0:T(8,128)(2,1)} copy-done((bf16[32,80,512]{2,1,0:T(8,128)(2,1)}, bf16[32,80,512]{2,1,0:T(8,128)(2,1)S(1)}, u32[]{:S(2)}) %copy-start) | copy-done | bytes 2621464
  79.7 7.4 %all-to-all-start.7 = ((bf16[32,80,512]{2,1,0:T(8,128)(2,1)}), bf16[32,80,512]{2,1,0:T(8,128)(2,1)S(1)}, u32[]{:S(2)}, u32[]{:S(2)}) async-start(bf16[32,80,512]{2,1,0:T(8,128)(2,1)} %bitcast.34), calls=%async_computation.7 | async-start | bytes 5242880 | tf_op jit(solution)/shard_map/all_to_all | solution.py:335
  87.3 1.7 %copy-done.1 = bf16[32,80,512]{2,1,0:T(8,128)(2,1)S(1)} copy-done((bf16[32,80,512]{2,1,0:T(8,128)(2,1)S(1)}, bf16[32,80,512]{2,1,0:T(8,128)(2,1)}, u32[]{:S(2)}) %copy-start.1) | copy-done | bytes 2621464
  89.0 3.4 %shard_map.107 = (bf16[128,512]{1,0:T(8,128)(2,1)S(1)}, bf16[128,512]{1,0:T(8,128)(2,1)S(1)}, bf16[128,512]{1,0:T(8,128)(2,1)S(1)}, bf16[128,512]{1,0:T(8,128)(2...) custom-call(s32[1,2560]{1,0:T(1,128)S(1)} %reshape.546.ids_ref, ...), custom_call_target="tpu_custom_call" | custom-call | flops 2684354560 | bytes 4000000 | tf_op jit(solution)/shard_map/pallas_call | solution.py:339
  92.4 1.2 collective-permute-start.13
  93.7 4.8 %collective-permute-start.11 = (bf16[128,512]{1,0:T(8,128)(2,1)}, bf16[128,512]{1,0:T(8,128)(2,1)}, u32[]{:S(2)}, u32[]{:S(2)}) collective-permute-start(bf16[128,512]{1,0:T(8,128)(2,1)} %get-tuple-element.224), channel_id=1, source_target_pairs={{0,40},{8,48},{16,56},{24,0},{32,8},{40,16},{48,24},{56,32},{1,41}... | collective-permute-start | bytes 393224 | tf_op jit(solution)/shard_map/ppermute | solution.py:348
  98.5 1.2 collective-permute-start.10
  99.7 2.7 %collective-permute-start.9 = (bf16[128,512]{1,0:T(8,128)(2,1)}, bf16[128,512]{1,0:T(8,128)(2,1)}, u32[]{:S(2)}, u32[]{:S(2)}) collective-permute-start(bf16[128,512]{1,0:T(8,128)(2,1)} %get-tuple-element.222), channel_id=1, source_target_pairs={{0,24},{8,32},{16,40},{24,48},{32,56},{40,0},{48,8},{56,16},{1,25}... | collective-permute-start | bytes 393224 | tf_op jit(solution)/shard_map/ppermute | solution.py:348
  102.4 0.7 collective-permute-start.8
  103.1 2.6 %collective-permute-done.12 = bf16[128,512]{1,0:T(8,128)(2,1)S(1)} collective-permute-done((bf16[128,512]{1,0:T(8,128)(2,1)S(1)}, bf16[128,512]{1,0:T(8,128)(2,1)S(1)}, u32[]{:S(2)}, u32[]{:S(2)}) %collective-permute-start.12) | collective-permute-done | bytes 131104 | tf_op jit(solution)/shard_map/ppermute | solution.py:348
  105.7 0.6 copy-done.10
  106.3 3.6 %collective-permute-start.7 = (bf16[128,512]{1,0:T(8,128)(2,1)S(1)}, bf16[128,512]{1,0:T(8,128)(2,1)}, u32[]{:S(2)}, u32[]{:S(2)}) collective-permute-start(bf16[128,512]{1,0:T(8,128)(2,1)S(1)} %get-tuple-element.220), channel_id=1, source_target_pairs={{0,8},{8,16},{16,24},{24,32},{32,40},{40,48},{48,56},{56,0},{1,9},... | collective-permute-start | bytes 393224 | tf_op jit(solution)/shard_map/ppermute | solution.py:348
  110.2 0.1 copy.68
  110.4 4.2 %collective-permute-done.11 = bf16[128,512]{1,0:T(8,128)(2,1)} collective-permute-done((bf16[128,512]{1,0:T(8,128)(2,1)}, bf16[128,512]{1,0:T(8,128)(2,1)}, u32[]{:S(2)}, u32[]{:S(2)}) %collective-permute-start.11) | collective-permute-done | bytes 131104 | tf_op jit(solution)/shard_map/ppermute | solution.py:348
  114.5 5.7 %collective-permute-done.9 = bf16[128,512]{1,0:T(8,128)(2,1)} collective-permute-done((bf16[128,512]{1,0:T(8,128)(2,1)}, bf16[128,512]{1,0:T(8,128)(2,1)}, u32[]{:S(2)}, u32[]{:S(2)}) %collective-permute-start.9) | collective-permute-done | bytes 131104 | tf_op jit(solution)/shard_map/ppermute | solution.py:348
  120.3 4.3 %collective-permute-done.7 = bf16[128,512]{1,0:T(8,128)(2,1)} collective-permute-done((bf16[128,512]{1,0:T(8,128)(2,1)S(1)}, bf16[128,512]{1,0:T(8,128)(2,1)}, u32[]{:S(2)}, u32[]{:S(2)}) %collective-permute-start.7) | collective-permute-done | bytes 131104 | tf_op jit(solution)/shard_map/ppermute | solution.py:348
  124.5 2.5 %subtract_convert_fusion.1 = (bf16[128,512]{1,0:T(8,128)(2,1)S(1)}, f32[128,512]{1,0:T(8,128)}, f32[128,512]{1,0:T(8,128)}, f32[128,512]{1,0:T(8,128)S(1)}) fusion(f32[128,512]{1,0:T(8,128)} %param.13, f32[128,512]{1,0:T(8,128)} %param.14, bf16[128,512]{1,0:T(8,128)(2,1)} %copy-done.9, bf16[128,512]{1,0:T(8,128)(2,1)} %copy-done.10, ...), kind=kLoop, calls=%fused_computation.89 | loop fusion | flops 1966080 | bytes 2621444 | tf_op jit(solution)/shard_map/convert_element_type | solution.py:32
  127.0 0.2 collective-permute-start.14
  127.3 2.7 %collective-permute-start.15 = (bf16[128,512]{1,0:T(8,128)(2,1)S(1)}, bf16[128,512]{1,0:T(8,128)(2,1)S(1)}, u32[]{:S(2)}, u32[]{:S(2)}) collective-permute-start(bf16[128,512]{1,0:T(8,128)(2,1)S(1)} %get-tuple-element.273), channel_id=1, source_target_pairs={{0,2},{1,3},{2,0},{3,1},{4,6},{5,7},{6,4},{7,5},{8,10},{9,11},{10,... | collective-permute-start | bytes 393224 | tf_op jit(solution)/shard_map/ppermute | solution.py:359
  129.9 1.8 %collective-permute-start.16 = (bf16[128,512]{1,0:T(8,128)(2,1)S(1)}, bf16[128,512]{1,0:T(8,128)(2,1)}, u32[]{:S(2)}, u32[]{:S(2)}) collective-permute-start(bf16[128,512]{1,0:T(8,128)(2,1)S(1)} %get-tuple-element.273), channel_id=1, source_target_pairs={{0,1},{1,2},{2,3},{3,0},{4,5},{5,6},{6,7},{7,4},{8,9},{9,10},{10,1... | collective-permute-start | bytes 393224 | tf_op jit(solution)/shard_map/ppermute | solution.py:359
  131.7 0.5 slice.28
  132.9 11.9 %shard_map.108 = bf16[320,2048]{1,0:T(8,128)(2,1)} custom-call(s32[320,4]{1,0:T(8,128)S(1)} %bitcast.89, s32[320,4]{1,0:T(8,128)S(1)} %negate_select_fusion.8.pcol_ref, f32[320,4]{1,0:T(8,128)S(1)} %copy.69.wcol_ref, bf16[2560,512]{1,0:T(8,128)(2,1)S(1)} %bitcast.86, bf16[4,512,2048]{2,1,0:T(8,128)(2,1)} %proj_ref.3), custom_call_target="tpu_custom_call" | custom-call | flops 6039797760 | bytes 13000000 | tf_op jit(solution)/shard_map/pallas_call | solution.py:365
  144.9 1.9 %conditional.1 = (bf16[320,2048]{1,0:T(8,128)(2,1)}, f32[128,512]{1,0:T(8,128)}, f32[128,512]{1,0:T(8,128)}, bf16[512,512]{1,0:T(8,128)(2,1)S(1)}) conditional(s32[]{:T(128)} %bitcast.32, (s32[]{:T(128)}, s32[4,1,1]{0,2,1:T(1,128)S(1)}, bf16[128,512]{1,0:T(8,128)(2,1)S(1)}, s32[]{:T(128)}, s32[4,1,1]{0,2,1:T(1,128)S(1)}, ...), branch_computations={%region_0.1_spmd, %region_1.10_spmd} | conditional | flops 5392232960 | bytes 94147792 | solution.py:389
  145.2 1.2 fusion.2
  146.7 0.8 copy.85
  (40 shorter events, 1.0 us)
Async XLA Ops:
  2.6 22.4 %all-to-all-start.5 = ((s32[32,1,128]{2,1,0:T(1,128)}), s32[32,1,128]{2,1,0:T(1,128)S(1)}, u32[]{:S(2)}, u32[]{:S(2)}) async-start(s32[32,1,128]{2,1,0:T(1,128)} %bitcast.27), calls=%async_computation.5 | async-start | bytes 32768 | tf_op jit(solution)/shard_map/all_to_all | solution.py:282
  23.4 1.6 %copy-start.2 = (bf16[2560,512]{1,0:T(8,128)(2,1)}, bf16[2560,512]{1,0:T(8,128)(2,1)S(1)}, u32[]{:S(2)}) copy-start(bf16[2560,512]{1,0:T(8,128)(2,1)S(1)} %shard_map.105) | copy-start | bytes 7864324
  25.0 53.1 %all-to-all-start.6 = ((bf16[32,80,512]{2,1,0:T(8,128)(2,1)}), bf16[32,80,512]{2,1,0:T(8,128)(2,1)S(1)}, u32[]{:S(2)}, u32[]{:S(2)}) async-start(bf16[32,80,512]{2,1,0:T(8,128)(2,1)} %bitcast.88), calls=%async_computation.6 | async-start | bytes 5242880 | tf_op jit(solution)/shard_map/all_to_all | solution.py:309
  33.3 12.9 %collective-permute-start = (bf16[128,512]{1,0:T(8,128)(2,1)S(1)}, bf16[128,512]{1,0:T(8,128)(2,1)S(1)}, u32[]{:S(2)}, u32[]{:S(2)}) collective-permute-start(bf16[128,512]{1,0:T(8,128)(2,1)S(1)} %constant_dynamic-slice_fusion.refs_0_), channel_id=1, source_target_pairs={{0,56},{8,0},{16,8},{24,16},{32,24},{40,32},{48,40},{56,48},{1,57}... | collective-permute-start | bytes 393224 | tf_op jit(solution)/shard_map/ppermute | solution.py:314
  39.3 10.8 %collective-permute-start.1 = (bf16[128,512]{1,0:T(8,128)(2,1)S(1)}, bf16[128,512]{1,0:T(8,128)(2,1)S(1)}, u32[]{:S(2)}, u32[]{:S(2)}) collective-permute-start(bf16[128,512]{1,0:T(8,128)(2,1)S(1)} %constant_dynamic-slice_fusion.refs_0_), channel_id=1, source_target_pairs={{0,48},{8,56},{16,0},{24,8},{32,16},{40,24},{48,32},{56,40},{1,49}... | collective-permute-start | bytes 393224 | tf_op jit(solution)/shard_map/ppermute | solution.py:314
  40.7 21.3 %collective-permute-start.2 = (bf16[128,512]{1,0:T(8,128)(2,1)S(1)}, bf16[128,512]{1,0:T(8,128)(2,1)S(1)}, u32[]{:S(2)}, u32[]{:S(2)}) collective-permute-start(bf16[128,512]{1,0:T(8,128)(2,1)S(1)} %constant_dynamic-slice_fusion.refs_0_), channel_id=1, source_target_pairs={{0,40},{8,48},{16,56},{24,0},{32,8},{40,16},{48,24},{56,32},{1,41}... | collective-permute-start | bytes 393224 | tf_op jit(solution)/shard_map/ppermute | solution.py:314
  41.2 20.9 %collective-permute-start.3 = (bf16[128,512]{1,0:T(8,128)(2,1)S(1)}, bf16[128,512]{1,0:T(8,128)(2,1)S(1)}, u32[]{:S(2)}, u32[]{:S(2)}) collective-permute-start(bf16[128,512]{1,0:T(8,128)(2,1)S(1)} %constant_dynamic-slice_fusion.refs_0_), channel_id=1, source_target_pairs={{0,32},{8,40},{16,48},{24,56},{32,0},{40,8},{48,16},{56,24},{1,33}... | collective-permute-start | bytes 393224 | tf_op jit(solution)/shard_map/ppermute | solution.py:314
  46.2 18.7 %collective-permute-start.4 = (bf16[128,512]{1,0:T(8,128)(2,1)S(1)}, bf16[128,512]{1,0:T(8,128)(2,1)}, u32[]{:S(2)}, u32[]{:S(2)}) collective-permute-start(bf16[128,512]{1,0:T(8,128)(2,1)S(1)} %constant_dynamic-slice_fusion.refs_0_), channel_id=1, source_target_pairs={{0,24},{8,32},{16,40},{24,48},{32,56},{40,0},{48,8},{56,16},{1,25}... | collective-permute-start | bytes 393224 | tf_op jit(solution)/shard_map/ppermute | solution.py:314
  46.2 21.6 %collective-permute-start.5 = (bf16[128,512]{1,0:T(8,128)(2,1)S(1)}, bf16[128,512]{1,0:T(8,128)(2,1)}, u32[]{:S(2)}, u32[]{:S(2)}) collective-permute-start(bf16[128,512]{1,0:T(8,128)(2,1)S(1)} %constant_dynamic-slice_fusion.refs_0_), channel_id=1, source_target_pairs={{0,16},{8,24},{16,32},{24,40},{32,48},{40,56},{48,0},{56,8},{1,17}... | collective-permute-start | bytes 393224 | tf_op jit(solution)/shard_map/ppermute | solution.py:314
  50.0 19.7 %collective-permute-start.6 = (bf16[128,512]{1,0:T(8,128)(2,1)S(1)}, bf16[128,512]{1,0:T(8,128)(2,1)}, u32[]{:S(2)}, u32[]{:S(2)}) collective-permute-start(bf16[128,512]{1,0:T(8,128)(2,1)S(1)} %constant_dynamic-slice_fusion.refs_0_), channel_id=1, source_target_pairs={{0,8},{8,16},{16,24},{24,32},{32,40},{40,48},{48,56},{56,0},{1,9},... | collective-permute-start | bytes 393224 | tf_op jit(solution)/shard_map/ppermute | solution.py:314
  69.7 1.3 copy-start.3
  78.1 1.6 %copy-start = (bf16[32,80,512]{2,1,0:T(8,128)(2,1)}, bf16[32,80,512]{2,1,0:T(8,128)(2,1)S(1)}, u32[]{:S(2)}) copy-start(bf16[32,80,512]{2,1,0:T(8,128)(2,1)S(1)} %all-to-all-done.6) | copy-start | bytes 7864324
  79.7 53.2 %all-to-all-start.7 = ((bf16[32,80,512]{2,1,0:T(8,128)(2,1)}), bf16[32,80,512]{2,1,0:T(8,128)(2,1)S(1)}, u32[]{:S(2)}, u32[]{:S(2)}) async-start(bf16[32,80,512]{2,1,0:T(8,128)(2,1)} %bitcast.34), calls=%async_computation.7 | async-start | bytes 5242880 | tf_op jit(solution)/shard_map/all_to_all | solution.py:335
  87.3 1.7 %copy-start.1 = (bf16[32,80,512]{2,1,0:T(8,128)(2,1)S(1)}, bf16[32,80,512]{2,1,0:T(8,128)(2,1)}, u32[]{:S(2)}) copy-start(bf16[32,80,512]{2,1,0:T(8,128)(2,1)} %copy-done) | copy-start | bytes 7864324
  89.0 21.0 %copy-start.12 = (bf16[320,4]{0,1:T(4,128)(2,1)S(1)}, bf16[320,4]{0,1:T(4,128)(2,1)}, u32[]{:S(2)}) copy-start(bf16[320,4]{0,1:T(4,128)(2,1)} %param.10) | copy-start | bytes 7684
  92.4 10.0 %collective-permute-start.13 = (bf16[128,512]{1,0:T(8,128)(2,1)S(1)}, bf16[128,512]{1,0:T(8,128)(2,1)S(1)}, u32[]{:S(2)}, u32[]{:S(2)}) collective-permute-start(bf16[128,512]{1,0:T(8,128)(2,1)S(1)} %get-tuple-element.226), channel_id=1, source_target_pairs={{0,56},{8,0},{16,8},{24,16},{32,24},{40,32},{48,40},{56,48},{1,57}... | collective-permute-start | bytes 393224 | tf_op jit(solution)/shard_map/ppermute | solution.py:348
  93.6 12.1 %collective-permute-start.12 = (bf16[128,512]{1,0:T(8,128)(2,1)S(1)}, bf16[128,512]{1,0:T(8,128)(2,1)S(1)}, u32[]{:S(2)}, u32[]{:S(2)}) collective-permute-start(bf16[128,512]{1,0:T(8,128)(2,1)S(1)} %get-tuple-element.225), channel_id=1, source_target_pairs={{0,48},{8,56},{16,0},{24,8},{32,16},{40,24},{48,32},{56,40},{1,49}... | collective-permute-start | bytes 393224 | tf_op jit(solution)/shard_map/ppermute | solution.py:348
  93.7 20.8 %collective-permute-start.11 = (bf16[128,512]{1,0:T(8,128)(2,1)}, bf16[128,512]{1,0:T(8,128)(2,1)}, u32[]{:S(2)}, u32[]{:S(2)}) collective-permute-start(bf16[128,512]{1,0:T(8,128)(2,1)} %get-tuple-element.224), channel_id=1, source_target_pairs={{0,40},{8,48},{16,56},{24,0},{32,8},{40,16},{48,24},{56,32},{1,41}... | collective-permute-start | bytes 393224 | tf_op jit(solution)/shard_map/ppermute | solution.py:348
  98.5 16.0 %collective-permute-start.10 = (bf16[128,512]{1,0:T(8,128)(2,1)}, bf16[128,512]{1,0:T(8,128)(2,1)}, u32[]{:S(2)}, u32[]{:S(2)}) collective-permute-start(bf16[128,512]{1,0:T(8,128)(2,1)} %get-tuple-element.223), channel_id=1, source_target_pairs={{0,32},{8,40},{16,48},{24,56},{32,0},{40,8},{48,16},{56,24},{1,33}... | collective-permute-start | bytes 393224 | tf_op jit(solution)/shard_map/ppermute | solution.py:348
  99.7 20.5 %collective-permute-start.9 = (bf16[128,512]{1,0:T(8,128)(2,1)}, bf16[128,512]{1,0:T(8,128)(2,1)}, u32[]{:S(2)}, u32[]{:S(2)}) collective-permute-start(bf16[128,512]{1,0:T(8,128)(2,1)} %get-tuple-element.222), channel_id=1, source_target_pairs={{0,24},{8,32},{16,40},{24,48},{32,56},{40,0},{48,8},{56,16},{1,25}... | collective-permute-start | bytes 393224 | tf_op jit(solution)/shard_map/ppermute | solution.py:348
  102.4 3.3 %copy-start.9 = (bf16[128,512]{1,0:T(8,128)(2,1)}, bf16[128,512]{1,0:T(8,128)(2,1)S(1)}, u32[]{:S(2)}) copy-start(bf16[128,512]{1,0:T(8,128)(2,1)S(1)} %collective-permute-done.13) | copy-start | bytes 393220
  102.4 17.8 %collective-permute-start.8 = (bf16[128,512]{1,0:T(8,128)(2,1)S(1)}, bf16[128,512]{1,0:T(8,128)(2,1)}, u32[]{:S(2)}, u32[]{:S(2)}) collective-permute-start(bf16[128,512]{1,0:T(8,128)(2,1)S(1)} %get-tuple-element.221), channel_id=1, source_target_pairs={{0,16},{8,24},{16,32},{24,40},{32,48},{40,56},{48,0},{56,8},{1,17}... | collective-permute-start | bytes 393224 | tf_op jit(solution)/shard_map/ppermute | solution.py:348
  105.7 0.7 copy-start.10
  106.3 18.2 %collective-permute-start.7 = (bf16[128,512]{1,0:T(8,128)(2,1)S(1)}, bf16[128,512]{1,0:T(8,128)(2,1)}, u32[]{:S(2)}, u32[]{:S(2)}) collective-permute-start(bf16[128,512]{1,0:T(8,128)(2,1)S(1)} %get-tuple-element.220), channel_id=1, source_target_pairs={{0,8},{8,16},{16,24},{24,32},{32,40},{40,48},{48,56},{56,0},{1,9},... | collective-permute-start | bytes 393224 | tf_op jit(solution)/shard_map/ppermute | solution.py:348
  127.0 17.8 %collective-permute-start.14 = (bf16[128,512]{1,0:T(8,128)(2,1)S(1)}, bf16[128,512]{1,0:T(8,128)(2,1)S(1)}, u32[]{:S(2)}, u32[]{:S(2)}) collective-permute-start(bf16[128,512]{1,0:T(8,128)(2,1)S(1)} %get-tuple-element.273), channel_id=1, source_target_pairs={{0,3},{1,0},{2,1},{3,2},{4,7},{5,4},{6,5},{7,6},{8,11},{9,8},{10,9... | collective-permute-start | bytes 393224 | tf_op jit(solution)/shard_map/ppermute | solution.py:359
  127.3 17.6 %collective-permute-start.15 = (bf16[128,512]{1,0:T(8,128)(2,1)S(1)}, bf16[128,512]{1,0:T(8,128)(2,1)S(1)}, u32[]{:S(2)}, u32[]{:S(2)}) collective-permute-start(bf16[128,512]{1,0:T(8,128)(2,1)S(1)} %get-tuple-element.273), channel_id=1, source_target_pairs={{0,2},{1,3},{2,0},{3,1},{4,6},{5,7},{6,4},{7,5},{8,10},{9,11},{10,... | collective-permute-start | bytes 393224 | tf_op jit(solution)/shard_map/ppermute | solution.py:359
  129.9 14.9 %collective-permute-start.16 = (bf16[128,512]{1,0:T(8,128)(2,1)S(1)}, bf16[128,512]{1,0:T(8,128)(2,1)}, u32[]{:S(2)}, u32[]{:S(2)}) collective-permute-start(bf16[128,512]{1,0:T(8,128)(2,1)S(1)} %get-tuple-element.273), channel_id=1, source_target_pairs={{0,1},{1,2},{2,3},{3,0},{4,5},{5,6},{6,7},{7,4},{8,9},{9,10},{10,1... | collective-permute-start | bytes 393224 | tf_op jit(solution)/shard_map/ppermute | solution.py:359
  132.9 12.0 %copy-start.11 = (s32[320,4]{0,1:T(4,128)S(1)}, s32[320,4]{0,1:T(4,128)}, u32[]{:S(2)}) copy-start(s32[320,4]{0,1:T(4,128)} %param.9) | copy-start | bytes 15364
